TPU v7x, 32 devices: a whole 2x2x4 slice. The times are simulated.
32 devices in a mesh: grp: 2 (over core), dp: 16 (over z, y, x), mp: 1.
Axes of the slice: x: 2, y: 2, z: 4, core: 2. Of those that a mesh axis runs over, the one named last changes fastest.
Arguments:
- states: bfloat16 [2, 32, 128, 4096], P('grp', 'dp'), may hold values from -6 to 6
- loss_grad: bfloat16 [32, 128, 4096], P('dp'), may hold values from -6 to 6
- gains: float32 [2, 4096], P('grp'), may hold values from 0.25 to 1.75
- w_param: bfloat16 [2, 4096, 2048], P('grp', 'dp', 'mp'), may hold values from -0.0234375 to 0.0234375, as said below
- w_fixed: bfloat16 [2, 4096, 2048], P('grp', 'dp', 'mp'), may hold values from -0.09375 to 0.09375
- probes: bfloat16 [2, 4096, 2, 2048], P('grp', 'dp', None, 'mp'), may hold values from -0.0234375 to 0.0234375, as said below
Outputs:
- hv: bfloat16 [2, 4096, 2, 2048], P('grp', 'dp', None, 'mp')
Inputs may be any that keep to these rules, and one draw needn't show every extreme that they name: `w_param`: independent entries of mean 0. `probes`: independent entries of mean 0.
All inputs are finite; a program needn't handle non-finite values.
Results may differ from a plain program's by a relative error of at most 0.025.
Values may be sent and summed in bfloat16 or wider, within the bound.
A program may use at most 128 MiB of HBM per device.

v0:
```python
import jax
import jax.numpy as jnp
from jax import lax
from jax.sharding import PartitionSpec as P

HEAD = 256


EPS = 1e-06


def passed_along(value, axis, steps):
    count = lax.axis_size(axis)
    first, last = (max(0, -steps), min(count, count - steps))
    return lax.ppermute(value, axis, [(source, source + steps) for source in range(first, last)])


def normalize(rows, gain):
    values = rows.astype(jnp.float32)
    scale = lax.rsqrt(jnp.mean(values * values, axis=-1, keepdims=True) + EPS)
    return (values * scale * gain).astype(jnp.bfloat16)


def attention_loss(query, keys, values, out_grad, scale, weight):
    scores = jnp.einsum("sihe,sjhe->shij", query, keys) * scale
    probs = jax.nn.softmax(scores, axis=-1)
    mixing = jnp.einsum("sihe,sjhe->shij", out_grad, values)
    return jnp.sum(probs * mixing) * weight


def curvature(query, keys, values, out_grad, t_query, t_keys, scale, weight):

    def grads(q_arg, k_arg):
        return jax.grad(attention_loss, argnums=(0, 1))(
            q_arg, k_arg, values, out_grad, scale, weight
        )

    def along(a_dir, b_dir):
        return jax.jvp(grads, (query, keys), (a_dir, b_dir))[1]

    return jax.vmap(along)(t_query, t_keys)


def shards(states, loss_grad, gains, w_param, w_fixed, probes):
    is_encoder = lax.axis_index("grp") == 0
    seqs_here = states.shape[1]
    length = states.shape[2]
    width = states.shape[3]
    rows = seqs_here * length
    cols = w_param.shape[2]
    probe_count = probes.shape[2]
    heads_here = cols // HEAD
    normed = normalize(states[0].reshape(rows, width), gains[0])
    source = jnp.where(is_encoder, normed, loss_grad.reshape(rows, width))
    first = jnp.dot(
        normed,
        lax.all_gather(w_param[0], "dp", axis=0, tiled=True),
        preferred_element_type=jnp.float32,
    )
    second = jnp.dot(
        source,
        lax.all_gather(w_fixed[0], "dp", axis=0, tiled=True),
        preferred_element_type=jnp.float32,
    )
    tang_acc = jnp.einsum(
        "rd,dpe->rpe",
        normed,
        lax.all_gather(probes[0], "dp", axis=0, tiled=True),
        preferred_element_type=jnp.float32,
    )
    projected = first.astype(jnp.bfloat16)
    other_side = second.astype(jnp.bfloat16)
    tangents = tang_acc.astype(jnp.bfloat16)
    keys, key_tangents, values = passed_along((projected, tangents, other_side), "grp", 1)

    def heads_of(x):
        return x.astype(jnp.float32).reshape(seqs_here, length, heads_here, HEAD)

    def probe_heads(x):
        return jnp.moveaxis(
            x.astype(jnp.float32).reshape(seqs_here, length, probe_count, heads_here, HEAD), 2, 0
        )

    def back_rows(x):
        return jnp.moveaxis(x, 0, 2).reshape(rows, probe_count, cols).astype(jnp.bfloat16)

    scale = 1.0
    weight = float(rows * lax.axis_size("dp")) ** (-0.5)
    d_query, d_keys = curvature(
        heads_of(projected),
        heads_of(keys),
        heads_of(values),
        heads_of(other_side),
        probe_heads(tangents),
        probe_heads(key_tangents),
        scale,
        weight,
    )
    d_query = back_rows(d_query)
    d_keys = back_rows(d_keys)
    returned = passed_along(d_keys, "grp", -1)
    chosen = jnp.where(is_encoder, returned, d_query)
    summed = lax.psum_scatter(
        jnp.einsum("rd,rpe->dpe", normed, chosen, preferred_element_type=jnp.float32).astype(
            jnp.bfloat16
        ),
        "dp",
        scatter_dimension=0,
        tiled=True,
    )
    return summed[None]


def solution(mesh):
    in_specs = (
        P("grp", "dp", None, None),
        P("dp", None, None),
        P("grp", None),
        P("grp", "dp", "mp"),
        P("grp", "dp", "mp"),
        P("grp", "dp", None, "mp"),
    )
    out_specs = P("grp", "dp", None, "mp")
    return jax.shard_map(shards, mesh=mesh, in_specs=in_specs, out_specs=out_specs, check_vma=False)
```

profile of v0, /device:TPU:0, one launch (start us, length us, event | category | flops | bytes accessed | tf_op | source)
XLA Modules:
  0.0 1526.4 jit_solution(10067214327612461618)
XLA Ops:
  8.1 3.8 copy.25
  11.9 1.5 copy-done.11
  13.4 3.0 copy.24
  16.4 4.1 copy.33
  21.2 2.9 multiply_convert_fusion
  24.1 180.3 %all-gather.9.cloned.1.call-done = bf16[1,4096,2048]{2,1,0:T(8,128)(2,1)} async-done(((bf16[1,256,2048]{2,1,0:T(8,128)(2,1)}), bf16[1,4096,2048]{2,1,0:T(8,128)(2,1)}) %all-gather.9.cloned.1.call-update) | async-done | bytes 16777232 | tf_op jit(solution)/shard_map/all_gather | solution.py:57
  204.5 8.3 fusion.11
  212.8 2.3 collective-permute-start
  215.1 182.0 %all-gather.11.cloned.1.call-done = bf16[1,4096,2048]{2,1,0:T(8,128)(2,1)} async-done(((bf16[1,256,2048]{2,1,0:T(8,128)(2,1)}), bf16[1,4096,2048]{2,1,0:T(8,128)(2,1)}) %all-gather.11.cloned.1.call-update) | async-done | bytes 16777232 | tf_op jit(solution)/shard_map/all_gather | solution.py:62
  397.1 10.3 fusion.14
  407.4 2.2 collective-permute-start.2
  409.9 1.4 copy.66
  411.3 1.1 bitcast_bitcast_fusion
  412.3 1.5 copy.63
  413.9 1.3 copy.67
  415.2 333.6 %all-gather.7.cloned.1.call-done = bf16[1,4096,2,2048]{3,1,2,0:T(8,128)(2,1)} async-done(((bf16[1,256,2,2048]{3,1,2,0:T(8,128)(2,1)}), bf16[1,4096,2,2048]{3,1,2,0:T(8,128)(2,1)}) %all-gather.7.cloned.1.call-update) | async-done | bytes 33554448 | tf_op jit(solution)/shard_map/all_gather | solution.py:68
  748.8 15.5 %fusion.8 = bf16[256,2,2048]{2,0,1:T(8,128)(2,1)S(1)} fusion(bf16[1,4096,2,2048]{3,1,2,0:T(8,128)(2,1)} %all-gather.7.cloned.1.call-done, bf16[256,4096]{0,1:T(8,128)(2,1)S(1)} %multiply_convert_fusion), kind=kOutput, calls=%fused_computation.13 | convolution fusion | flops 8590983168 | bytes 37748736 | tf_op jit(solution)/shard_map/rd,dpe->rpe/dot_general | solution.py:65
  764.3 1.7 collective-permute-start.1
  766.5 1.1 fusion.70
  773.6 0.9 add_reduce_fusion
  775.0 2.9 fusion.37
  777.9 6.5 fusion.7
  784.4 4.1 copy.37
  788.5 4.3 convert_element_type.50
  792.7 1.5 collective-permute-start.3
  794.3 5.3 fusion.36
  799.6 6.4 fusion.6
  806.1 4.1 copy.41
  810.2 4.2 convert_element_type.52
  814.3 16.3 %convolution_convert_fusion = bf16[4096,2,2048]{2,0,1:T(8,128)(2,1)} fusion(bf16[256,4096]{0,1:T(8,128)(2,1)S(1)} %multiply_convert_fusion, bf16[256,2,2048]{2,0,1:T(8,128)(2,1)} %collective-permute-done.3, bf16[256,2,2048]{2,0,1:T(8,128)(2,1)} %convert_element_type.52, pred[]{:T(512)S(6)} %eq.3), kind=kOutput, calls=%fused_computation.2 | convolution fusion | flops 8607760384 | bytes 39845888 | tf_op jit(solution)/shard_map/rd,rpe->dpe/dot_general | solution.py:104
  830.6 684.1 %reduce-scatter.2.cloned.1.call-done = bf16[256,2,2048]{2,0,1:T(8,128)(2,1)} async-done(((bf16[4096,2,2048]{2,0,1:T(8,128)(2,1)}), bf16[256,2,2048]{2,0,1:T(8,128)(2,1)}) %reduce-scatter.2.cloned.1.call-update) | async-done | bytes 2097168 | tf_op jit(solution)/shard_map/reduce_scatter | solution.py:103
  1514.8 5.1 copy.42
  (58 shorter events, 9.4 us)
Async XLA Ops:
  6.5 197.9 %all-gather.9.cloned.1.call-start = ((), (), s32[]{:S(2)}) async-start(), calls=%async_computation.3 | async-start | bytes 17825792 | tf_op jit(solution)/shard_map/all_gather | solution.py:57
  7.3 389.8 %all-gather.11.cloned.1.call-start = ((), (), s32[]{:S(2)}) async-start(), calls=%async_computation.4 | async-start | bytes 17825792 | tf_op jit(solution)/shard_map/all_gather | solution.py:62
  8.0 740.8 %all-gather.7.cloned.1.call-start = ((), (), s32[]{:S(2)}) async-start(), calls=%async_computation.2 | async-start | bytes 35651584 | tf_op jit(solution)/shard_map/all_gather | solution.py:68
  11.8 1.6 copy-start.11
  11.9 1502.9 %reduce-scatter.2.cloned.1.call-start = ((), (), s32[]{:S(2)}) async-start(), calls=%async_computation.1 | async-start | bytes 35651584 | tf_op jit(solution)/shard_map/reduce_scatter | solution.py:103
  20.5 0.7 copy-start.15
  212.8 199.6 %collective-permute-start = (bf16[256,2048]{1,0:T(8,128)(2,1)S(1)}, bf16[256,2048]{1,0:T(8,128)(2,1)}, u32[]{:S(2)}, u32[]{:S(2)}) collective-permute-start(bf16[256,2048]{1,0:T(8,128)(2,1)S(1)} %fusion.11), channel_id=1, source_target_pairs={{0,16},{1,17},{2,18},{3,19},{4,20},{5,21},{6,22},{7,23},{8,24},{9,... | collective-permute-start | bytes 3145736 | tf_op jit(solution)/shard_map/ppermute | solution.py:15
  407.4 6.5 collective-permute-start.2
  409.9 2.4 copy-start.8
  413.9 352.2 %copy-start.6 = (bf16[32,8,8,256]{3,2,1,0:T(8,128)(2,1)}, bf16[32,8,8,256]{3,2,1,0:T(8,128)(2,1)S(1)}, u32[]{:S(2)}) copy-start(bf16[32,8,8,256]{3,2,1,0:T(8,128)(2,1)S(1)} %copy.63) | copy-start | bytes 3145732
  748.8 17.2 %copy-start.9 = (bf16[32,8,8,256]{3,2,1,0:T(8,128)(2,1)S(1)}, bf16[32,8,8,256]{3,2,1,0:T(8,128)(2,1)}, u32[]{:S(2)}) copy-start(bf16[32,8,8,256]{3,2,1,0:T(8,128)(2,1)} %copy-done.8) | copy-start | bytes 3145732
  764.3 7.2 collective-permute-start.1
  766.0 1.6 copy-start.13
  766.1 1.8 copy-start.14
  766.5 1.9 copy-start.12
  767.9 1.2 copy-start.7
  769.2 1.1 copy-start.5
  769.4 5.1 copy-start.1
  769.4 5.1 copy-start.4
  770.1 1.4 copy-start.2
  771.5 1.2 copy-start.10
  772.2 1.4 copy-start.3
  773.6 1.4 copy-start
  792.7 21.6 %collective-permute-start.3 = (bf16[256,2,2048]{2,0,1:T(8,128)(2,1)}, bf16[256,2,2048]{2,0,1:T(8,128)(2,1)}, u32[]{:S(2)}, u32[]{:S(2)}) collective-permute-start(bf16[256,2,2048]{2,0,1:T(8,128)(2,1)} %convert_element_type.50), channel_id=1, source_target_pairs={{16,0},{17,1},{18,2},{19,3},{20,4},{21,5},{22,6},{23,7},{24,8},{25... | collective-permute-start | bytes 6291464 | tf_op jit(solution)/shard_map/ppermute | solution.py:15
Sparse Core Ops, SparseCore 0:
  10.1 194.3 all-gather.8
  207.2 189.7 all-gather.10
  399.8 348.9 all-gather.6
  830.8 683.9 reduce-scatter.1
where the time goes:
time: 1530 us
  waiting for transfers between devices  1380 us (90%)
  matrix products  74.1 us (5%)
  local copies, waits for them, and re-layouts  43.7 us (3%)
    reduce_scatter x1, waiting for transfers between devices, shards(): lax.psum_scatter(jnp.einsum('rd,rpe->dpe', normed, chosen, preferred_elem...  684 us
    all_gather x1, waiting for transfers between devices, shards(): lax.all_gather(probes[0], 'dp', axis=0, tiled=True)  334 us
    all_gather x1, waiting for transfers between devices, shards(): lax.all_gather(w_fixed[0], 'dp', axis=0, tiled=True)  182 us
    all_gather x1, waiting for transfers between devices, shards(): lax.all_gather(w_param[0], 'dp', axis=0, tiled=True)  180 us
  transfers between devices with their start and end apart: 8, of which 4 were waited for; matrix products, arithmetic and copies ran while one was open for 4% of the time, Pallas kernels for 0%

commit v1 on v0

v1 whole, which is shorter than its diff:
```python
import jax
import jax.numpy as jnp
from jax import lax
from jax.sharding import Mesh, PartitionSpec as P

HEAD = 256


EPS = 1e-06


def normalize(rows, gain):
    values = rows.astype(jnp.float32)
    scale = lax.rsqrt(jnp.mean(values * values, axis=-1, keepdims=True) + EPS)
    return (values * scale * gain).astype(jnp.bfloat16)


def passed_along(value, axis, steps):
    count = lax.axis_size(axis)
    first, last = (max(0, -steps), min(count, count - steps))
    return lax.ppermute(value, axis, [(source, source + steps) for source in range(first, last)])


def attention_loss(query, keys, values, out_grad, weight):
    scores = jnp.einsum("sihe,sjhe->shij", query, keys)
    probs = jax.nn.softmax(scores, axis=-1)
    mixing = jnp.einsum("sihe,sjhe->shij", out_grad, values)
    return jnp.sum(probs * mixing) * weight


def curvature(query, keys, values, out_grad, t_query, t_keys, weight):

    def grads(q_arg, k_arg):
        return jax.grad(attention_loss, argnums=(0, 1))(q_arg, k_arg, values, out_grad, weight)

    def along(a_dir, b_dir):
        return jax.jvp(grads, (query, keys), (a_dir, b_dir))[1]

    return jax.vmap(along)(t_query, t_keys)


def split(dp, heads_here):
    cols = 1
    while cols < 4 and dp % (cols * 2) == 0 and heads_here % (cols * 2) == 0:
        cols *= 2
    return cols, dp // cols


def shards(states, loss_grad, gains, w_param, w_fixed, probes):
    ncol = lax.axis_size("c")
    nrow = lax.axis_size("r")
    is_encoder = lax.axis_index("grp") == 0
    seqs_own, length, width = states.shape[1:]
    rows_own = seqs_own * length
    depth = w_param.shape[1]
    cols_mp = w_param.shape[2]
    cols = cols_mp // ncol
    probe_count = probes.shape[2]
    heads = cols // HEAD
    rows = rows_own * ncol
    seqs = seqs_own * ncol

    normed_own = normalize(states[0].reshape(rows_own, width), gains[0])
    def reorder(x):
        x = x.reshape(rows_own, ncol, nrow, depth)
        return jnp.swapaxes(x, 1, 2).reshape(rows_own, width)

    normed_own = reorder(normed_own)
    source_own = jnp.where(is_encoder, normed_own, reorder(loss_grad))

    wcat = jnp.concatenate([w_param[0][:, None], probes[0], w_fixed[0][:, None]], axis=1)
    wcat = wcat.reshape(depth, 2 + probe_count, ncol, cols)
    wcat = jnp.transpose(wcat, (2, 0, 1, 3)).reshape(ncol, depth, (2 + probe_count) * cols)
    mine = lax.all_to_all(wcat, "c", split_axis=0, concat_axis=0, tiled=True)
    mine = mine.reshape(ncol * depth, (2 + probe_count) * cols)
    w_all = lax.all_gather(mine, "r", axis=0, tiled=True)

    normed = lax.all_gather(normed_own, "c", axis=0, tiled=True)
    source = lax.all_gather(source_own, "c", axis=0, tiled=True)
    wide = (1 + probe_count) * cols
    first = jnp.dot(normed, w_all[:, :wide], preferred_element_type=jnp.float32).astype(jnp.bfloat16)
    second = jnp.dot(source, w_all[:, wide:], preferred_element_type=jnp.float32).astype(jnp.bfloat16)

    k_first, k_second = passed_along((first, second), "grp", 1)

    def heads_of(x):
        return x.astype(jnp.float32).reshape(seqs, length, heads, HEAD)

    def probe_heads(x):
        return jnp.moveaxis(
            x.astype(jnp.float32).reshape(seqs, length, probe_count, heads, HEAD), 2, 0
        )

    def back_rows(x):
        return jnp.moveaxis(x, 0, 2).reshape(rows, probe_count * cols).astype(jnp.bfloat16)

    weight = float(rows_own * ncol * nrow) ** (-0.5)
    d_query, d_keys = curvature(
        heads_of(first[:, :cols]),
        heads_of(k_first[:, :cols]),
        heads_of(k_second),
        heads_of(second),
        probe_heads(first[:, cols:]),
        probe_heads(k_first[:, cols:]),
        weight,
    )
    d_query = back_rows(d_query)
    d_keys = back_rows(d_keys)
    returned = passed_along(d_keys, "grp", -1)
    chosen = jnp.where(is_encoder, returned, d_query)
    part = lax.dot_general(
        normed, chosen, (((0,), (0,)), ((), ())), preferred_element_type=jnp.float32
    ).astype(jnp.bfloat16)
    summed = lax.psum_scatter(part, "r", scatter_dimension=0, tiled=True)
    summed = summed.reshape(ncol, depth, probe_count * cols)
    out = lax.all_to_all(summed, "c", split_axis=0, concat_axis=0, tiled=True)
    out = jnp.transpose(out.reshape(ncol, depth, probe_count, cols), (1, 2, 0, 3))
    return out.reshape(1, depth, probe_count, cols_mp)


def solution(mesh):
    grp, dp, mp = (mesh.shape[name] for name in ("grp", "dp", "mp"))

    def run(states, loss_grad, gains, w_param, w_fixed, probes):
        ncol, nrow = split(dp, w_param.shape[2] // mp // HEAD)
        fine = Mesh(mesh.devices.reshape(grp, ncol, nrow, mp), ("grp", "c", "r", "mp"))
        in_specs = (
            P("grp", ("c", "r"), None, None),
            P(("c", "r"), None, None),
            P("grp", None),
            P("grp", ("c", "r"), "mp"),
            P("grp", ("c", "r"), "mp"),
            P("grp", ("c", "r"), None, "mp"),
        )
        out_specs = P("grp", ("c", "r"), None, "mp")
        return jax.shard_map(shards, mesh=fine, in_specs=in_specs, out_specs=out_specs, check_vma=False)(
            states, loss_grad, gains, w_param, w_fixed, probes
        )

    return run
```

time: 1530 us -> 821 us (0.54)
  waiting for transfers between devices: 1380 us -> 379 us
  blocking collectives: 0 us -> 262 us
  local copies, waits for them, and re-layouts: 43.7 us -> 79.9 us
    reduce_scatter x1, waiting for transfers between devices: 684 us -> 86.4 us  [shards(): summed = lax.psum_scatter(part, 'r', scatter_dimension=0, tiled=True)]
    all_gather x3, waiting for transfers between devices: 696 us -> 292 us  [the longest x1 159 us: shards(): w_all = lax.all_gather(mine, 'r', axis=0, tiled=True)]
    all_to_all x0 -> x2, blocking collectives: none -> 262 us  [the longest x1 210 us: shards(): mine = lax.all_to_all(wcat, 'c', split_axis=0, concat_axis=0, tiled=True)]
    reshape x3 -> x10, local copies, waits for them, and re-layouts: 5.2 us -> 27.4 us  [the longest x2 7.8 us: probe_heads(): x.astype(jnp.float32).reshape(seqs, length, probe_count, heads, HEAD)]
    dot_general x11 -> x10, matrix products: 73.6 us -> 64.3 us  [the longest x7 19.6 us: attention_loss(): scores = jnp.einsum('sihe,sjhe->shij', query, keys)]
  transfers between devices with their start and end apart: 8 -> 7, of which waited for: 4 -> 4; matrix products, arithmetic and copies ran while one was open for 4% -> 10% of each run, Pallas kernels for 0% -> 0%
where the time goes in v1:
time: 821 us; the launch traced here: 820 us
  waiting for transfers between devices  379 us (46%)
  blocking collectives  262 us (32%)
  local copies, waits for them, and re-layouts  79.9 us (10%)
  matrix products  64.8 us (8%)
  between operations  13.5 us (2%)
  other arithmetic  12.6 us (2%)
    all_to_all x1, blocking collectives, shards(): mine = lax.all_to_all(wcat, 'c', split_axis=0, concat_axis=0, tiled=True)  210 us
    all_gather x1, waiting for transfers between devices, shards(): w_all = lax.all_gather(mine, 'r', axis=0, tiled=True)  159 us
    all_gather x1, waiting for transfers between devices, shards(): source = lax.all_gather(source_own, 'c', axis=0, tiled=True)  128 us
    reduce_scatter x1, waiting for transfers between devices, shards(): summed = lax.psum_scatter(part, 'r', scatter_dimension=0, tiled=True)  86.4 us
    all_to_all x1, blocking collectives, shards(): out = lax.all_to_all(summed, 'c', split_axis=0, concat_axis=0, tiled=True)  52.8 us
    dot_general x7, matrix products, attention_loss(): scores = jnp.einsum('sihe,sjhe->shij', query, keys)  19.6 us
    dot_general x1, matrix products, shards(): jnp.dot(normed, w_all[:, :wide], preferred_element_type=jnp.float32)  19.3 us
    unnamed x43, local copies, waits for them, and re-layouts  17.4 us
  transfers between devices with their start and end apart: 7, of which 4 were waited for; matrix products, arithmetic and copies ran while one was open for 10% of the time, Pallas kernels for 0%

profile of v1, /device:TPU:0, one launch (start us, length us, event | category | flops | bytes accessed | tf_op | source)
XLA Modules:
  0.0 819.8 jit_solution(941999837300472358)
XLA Ops:
  8.8 4.6 reshape.141
  14.6 2.9 fusion.9
  17.5 2.7 copy.40
  23.3 4.7 copy.42
  29.9 209.6 %all_to_all.10 = bf16[4,256,2048]{1,2,0:T(8,128)(2,1)} all-to-all(bf16[4,256,2048]{1,2,0:T(8,128)(2,1)S(1)} %bitcast.92), channel_id=1, replica_groups=mesh['grp'=2,'c'=4,'r'=4,'mp'=1] {'c'}, dimensions={0} | all-to-all | bytes 8388608 | tf_op jit(solution)/shard_map/all_to_all | solution.py:74
  239.5 6.3 copy.45
  247.4 2.8 reshape.134
  250.2 4.4 copy.52
  254.7 3.1 bitcast_select_fusion.2
  257.9 4.8 all-gather.4.cloned.1.call-done
  262.7 159.5 %all-gather.6.cloned.1.call-done = bf16[4096,2048]{1,0:T(8,128)(2,1)} async-done(((bf16[1024,2048]{1,0:T(8,128)(2,1)}), bf16[4096,2048]{1,0:T(8,128)(2,1)}) %all-gather.6.cloned.1.call-update) | async-done | bytes 16777232 | tf_op jit(solution)/shard_map/all_gather | solution.py:76
  422.1 19.3 %fusion.6 = bf16[1024,1536]{1,0:T(8,128)(2,1)} fusion(bf16[1024,4096]{0,1:T(8,128)(2,1)} %all-gather.4.cloned.1.call-done, bf16[4096,2048]{1,0:T(8,128)(2,1)} %all-gather.6.cloned.1.call-done), kind=kOutput, calls=%fused_computation.12 | convolution fusion | flops 12886474752 | bytes 24117248 | tf_op jit(solution)/shard_map/dot_general | solution.py:81
  441.4 3.4 collective-permute-start
  444.8 128.1 %all-gather.8.cloned.1.call-done = bf16[1024,4096]{0,1:T(8,128)(2,1)} async-done(((bf16[256,4096]{0,1:T(8,128)(2,1)}), bf16[1024,4096]{0,1:T(8,128)(2,1)}) %all-gather.8.cloned.1.call-update) | async-done | bytes 8388624 | tf_op jit(solution)/shard_map/all_gather | solution.py:79
  572.9 10.1 %fusion.25 = bf16[1024,512]{1,0:T(8,128)(2,1)} fusion(bf16[1024,4096]{0,1:T(8,128)(2,1)} %all-gather.8.cloned.1.call-done, bf16[4096,2048]{1,0:T(8,128)(2,1)} %all-gather.6.cloned.1.call-done), kind=kOutput, calls=%fused_computation.34 | convolution fusion | flops 4295491584 | bytes 13631488 | tf_op jit(solution)/shard_map/dot_general | solution.py:82
  583.0 2.9 collective-permute-start.1
  589.4 3.1 slice.25
  593.6 3.3 reshape.130
  596.9 2.9 reshape.137
  599.8 3.1 slice.28
  602.9 4.5 reshape.133
  621.2 2.8 fusion.29
  624.0 5.9 fusion.5
  629.9 4.3 copy.56
  634.2 3.7 copy.129
  639.4 2.9 fusion.28
  642.4 4.6 fusion.4
  649.6 15.3 %convolution_convert_fusion = bf16[4096,1024]{1,0:T(8,128)(2,1)} fusion(bf16[1024,4096]{0,1:T(8,128)(2,1)} %all-gather.4.cloned.1.call-done, bf16[1024,1024]{0,1:T(8,128)(2,1)} %collective-permute-done.2, bf16[128,8,8,128]{3,2,1,0:T(8,128)(2,1)} %bitcast.101, pred[]{:T(512)S(6)} %eq.3), kind=kOutput, calls=%fused_computation.2 | convolution fusion | flops 8595177472 | bytes 20971520 | tf_op jit(solution)/shard_map/dot_general | solution.py:111
  664.9 86.4 %reduce-scatter.2.cloned.1.call-done = bf16[1024,1024]{1,0:T(8,128)(2,1)} async-done(((bf16[4096,1024]{1,0:T(8,128)(2,1)}), bf16[1024,1024]{1,0:T(8,128)(2,1)}) %reduce-scatter.2.cloned.1.call-update) | async-done | bytes 2097168 | tf_op jit(solution)/shard_map/reduce_scatter | solution.py:114
  751.3 52.8 %all_to_all.11 = bf16[4,256,1024]{2,1,0:T(8,128)(2,1)S(1)} all-to-all(bf16[4,256,1024]{2,1,0:T(8,128)(2,1)} %bitcast.102), channel_id=1, replica_groups=mesh['grp'=2,'c'=4,'r'=4,'mp'=1] {'c'}, dimensions={0} | all-to-all | bytes 4194304 | tf_op jit(solution)/shard_map/all_to_all | solution.py:116
  804.1 2.7 reshape.139
  806.8 4.3 copy.130
  (77 shorter events, 34.7 us)
Async XLA Ops:
  6.5 2.2 copy-start.11
  6.5 256.1 %all-gather.4.cloned.1.call-start = ((), (), s32[]{:S(2)}) async-start(), calls=%async_computation.3 | async-start | bytes 10485760 | tf_op jit(solution)/shard_map/all_gather | solution.py:78
  8.8 5.1 copy-start.18
  20.2 1.2 copy-start.16
  20.2 1.7 copy-start.17
  20.2 401.9 %all-gather.6.cloned.1.call-start = ((), (), s32[]{:S(2)}) async-start(), calls=%async_computation.4 | async-start | bytes 20971520 | tf_op jit(solution)/shard_map/all_gather | solution.py:76
  245.8 1.6 copy-start.15
  245.8 327.0 %all-gather.8.cloned.1.call-start = ((), (), s32[]{:S(2)}) async-start(), calls=%async_computation.5 | async-start | bytes 10485760 | tf_op jit(solution)/shard_map/all_gather | solution.py:79
  250.2 4.4 copy-start.2
  257.8 493.5 %reduce-scatter.2.cloned.1.call-start = ((), (), s32[]{:S(2)}) async-start(), calls=%async_computation.6 | async-start | bytes 10485760 | tf_op jit(solution)/shard_map/reduce_scatter | solution.py:114
  441.4 158.4 %collective-permute-start = (bf16[1024,1536]{1,0:T(8,128)(2,1)}, bf16[1024,1536]{1,0:T(8,128)(2,1)}, u32[]{:S(2)}, u32[]{:S(2)}) collective-permute-start(bf16[1024,1536]{1,0:T(8,128)(2,1)} %fusion.6), channel_id=1, source_target_pairs={{0,16},{1,17},{2,18},{3,19},{4,20},{5,21},{6,22},{7,23},{8,24},{9,... | collective-permute-start | bytes 9437192 | tf_op jit(solution)/shard_map/ppermute | solution.py:21
  583.0 13.9 %collective-permute-start.1 = (bf16[1024,512]{1,0:T(8,128)(2,1)}, bf16[1024,512]{1,0:T(8,128)(2,1)}, u32[]{:S(2)}, u32[]{:S(2)}) collective-permute-start(bf16[1024,512]{1,0:T(8,128)(2,1)} %fusion.25), channel_id=1, source_target_pairs={{0,16},{1,17},{2,18},{3,19},{4,20},{5,21},{6,22},{7,23},{8,24},{9,... | collective-permute-start | bytes 3145736 | tf_op jit(solution)/shard_map/ppermute | solution.py:21
  596.9 19.8 %copy-start.3 = (bf16[8,128,2,2,256]{4,3,2,1,0:T(2,128)(2,1)}, bf16[8,128,2,2,256]{4,3,2,1,0:T(2,128)(2,1)S(1)}, u32[]{:S(2)}) copy-start(bf16[8,128,2,2,256]{4,3,2,1,0:T(2,128)(2,1)S(1)} %reshape.130) | copy-start | bytes 6291460
  611.0 1.0 copy-start.7
  612.0 3.8 copy-start.13
  612.0 3.8 copy-start.14
  613.8 1.0 copy-start.12
  616.3 1.3 copy-start.8
  616.6 4.5 copy-start
  616.6 4.5 copy-start.5
  617.6 1.6 copy-start.4
  617.6 1.9 copy-start.10
  634.2 5.2 copy-start.1
  634.2 5.2 copy-start.6
  634.2 5.2 copy-start.9
  637.9 11.7 %collective-permute-start.2 = (bf16[1024,1024]{0,1:T(8,128)(2,1)}, bf16[1024,1024]{0,1:T(8,128)(2,1)}, u32[]{:S(2)}, u32[]{:S(2)}) collective-permute-start(bf16[1024,1024]{0,1:T(8,128)(2,1)} %bitcast.86), channel_id=1, source_target_pairs={{16,0},{17,1},{18,2},{19,3},{20,4},{21,5},{22,6},{23,7},{24,8},{25... | collective-permute-start | bytes 6291464 | tf_op jit(solution)/shard_map/ppermute | solution.py:21
Sparse Core Ops, SparseCore 0:
  20.4 242.2 all-gather.3
  264.5 157.5 all-gather.5
  423.7 149.1 all-gather.7
  665.0 86.2 reduce-scatter.1

commit v2 on v1

v2 whole, which is shorter than its diff:
```python
import functools

import jax
import jax.numpy as jnp
from jax import lax
from jax.experimental import pallas as pl
from jax.experimental.pallas import tpu as pltpu
from jax.sharding import PartitionSpec as P

HEAD = 256


EPS = 1e-06
MESH = pl.DeviceIdType.MESH


def normalize(rows, gain):
    values = rows.astype(jnp.float32)
    scale = lax.rsqrt(jnp.mean(values * values, axis=-1, keepdims=True) + EPS)
    return (values * scale * gain).astype(jnp.bfloat16)


def passed_along(value, axis, steps):
    count = lax.axis_size(axis)
    first, last = (max(0, -steps), min(count, count - steps))
    return lax.ppermute(value, axis, [(source, source + steps) for source in range(first, last)])


def attention_loss(query, keys, values, out_grad, weight):
    scores = jnp.einsum("sihe,sjhe->shij", query, keys)
    probs = jax.nn.softmax(scores, axis=-1)
    mixing = jnp.einsum("sihe,sjhe->shij", out_grad, values)
    return jnp.sum(probs * mixing) * weight


def curvature(query, keys, values, out_grad, t_query, t_keys, weight):

    def grads(q_arg, k_arg):
        return jax.grad(attention_loss, argnums=(0, 1))(q_arg, k_arg, values, out_grad, weight)

    def along(a_dir, b_dir):
        return jax.jvp(grads, (query, keys), (a_dir, b_dir))[1]

    return jax.vmap(along)(t_query, t_keys)


class Split:
    def __init__(self, dp, heads_here):
        bits = dp.bit_length() - 1
        assert dp == 1 << bits
        col = []
        for bit in range(0, bits, 2):
            if len(col) < 2 and heads_here % (2 << len(col)) == 0:
                col.append(1 << bit)
        self.col = col[::-1]
        self.row = [1 << bit for bit in reversed(range(bits)) if 1 << bit not in col]
        self.ncol = 1 << len(col)
        self.nrow = 1 << len(self.row)

    def col_mask(self, offset):
        return [b for i, b in enumerate(self.col) if (offset >> i) & 1]

    def row_mask(self, offset):
        return [b for i, b in enumerate(self.row) if (offset >> i) & 1]

    def col_index(self, index):
        return sum((((index // b) % 2) * (1 << i) for i, b in enumerate(self.col)), 0)


def flipped(index, masks):
    for b in masks:
        index = index + b - 2 * b * ((index // b) % 2)
    return index


def greet(me, split):
    peers = [split.col_mask(o) for o in range(1, split.ncol)] + [[b] for b in split.row]
    barrier = pltpu.get_barrier_semaphore()
    for masks in peers:
        pl.semaphore_signal(
            barrier, inc=1, device_id={"dp": flipped(me, masks)}, device_id_type=MESH
        )
    pl.semaphore_wait(barrier, len(peers))


def gather_kernel(split, pieces, w_ref, n_ref, g_ref, w_out, n_out, g_out,
                  w_send, w_recv, n_send, n_recv, g_send, g_recv, own_sem):
    me = lax.axis_index("dp")
    decoder = lax.axis_index("grp") != 0
    depth = w_ref.shape[1]
    ncol, nrow = split.ncol, split.nrow
    my_col = split.col_index(me)
    rows = n_ref.shape[0]
    piece = rows // pieces

    def weight_slot(cs, ro):
        source = flipped(flipped(me, split.col_mask(cs)), split.row_mask(ro))
        return w_out.at[pl.ds(pl.multiple_of(source * depth, depth), depth)]

    def row_slot(out, co, k):
        source = split.col_index(flipped(me, split.col_mask(co)))
        return out.at[pl.ds(pl.multiple_of(source * rows + k * piece, piece), piece)]

    def remote(src, dst, send, recv, masks):
        return pltpu.make_async_remote_copy(
            src_ref=src, dst_ref=dst, send_sem=send, recv_sem=recv,
            device_id={"dp": flipped(me, masks)}, device_id_type=MESH,
        )

    greet(me, split)

    sent = []
    gsent = []

    def weight_copy(cs, ro):
        if ro == 0:
            dest = split.col_index(flipped(me, split.col_mask(cs)))
            return remote(w_ref.at[dest], weight_slot(0, 0), w_send.at[cs, 0], w_recv.at[cs, 0],
                          split.col_mask(cs))
        stage = ro.bit_length() - 1
        held = ro - (1 << stage)
        src = w_ref.at[my_col] if (cs, held) == (0, 0) else weight_slot(cs, held)
        return remote(src, weight_slot(cs, held), w_send.at[cs, ro], w_recv.at[cs, ro],
                      [split.row[stage]])

    def row_copy(own, out, send, recv, co, k):
        stage = co.bit_length() - 1
        held = co - (1 << stage)
        src = own.at[pl.ds(k * piece, piece)] if held == 0 else row_slot(out, held, k)
        return remote(src, row_slot(out, held, k), send.at[co, k], recv.at[co, k],
                      [split.col[stage]])

    def start_weight(cs, ro):
        copy = weight_copy(cs, ro)
        copy.start()
        sent.append(copy)

    def start_row(co, k):
        copy = row_copy(n_ref, n_out, n_send, n_recv, co, k)
        copy.start()
        sent.append(copy)
        gcopy = row_copy(g_ref, g_out, g_send, g_recv, co, k)

        @pl.when(decoder)
        def _():
            gcopy.start()

        gsent.append(gcopy)

    row_stages = len(split.row)
    col_stages = len(split.col)

    def have_weight(cs, ro):
        first = ro.bit_length()
        for stage in range(first, row_stages):
            start_weight(cs, ro + (1 << stage))

    def have_row(co, k):
        for stage in range(co.bit_length(), col_stages):
            start_row(co + (1 << stage), k)

    for cs in range(1, ncol):
        start_weight(cs, 0)
    have_weight(0, 0)
    for k in range(pieces):
        have_row(0, k)

    own = [
        pltpu.make_async_copy(w_ref.at[my_col], weight_slot(0, 0), own_sem.at[0]),
        pltpu.make_async_copy(
            n_ref, n_out.at[pl.ds(pl.multiple_of(my_col * rows, rows), rows)], own_sem.at[1]
        ),
        pltpu.make_async_copy(
            g_ref, g_out.at[pl.ds(pl.multiple_of(my_col * rows, rows), rows)], own_sem.at[2]
        ),
    ]
    for copy in own:
        copy.start()

    weights = sorted(
        ((cs, ro) for cs in range(ncol) for ro in range(nrow) if (cs, ro) != (0, 0)),
        key=lambda b: (b[1].bit_length() + (1 if b[0] else 0), b[1], b[0]),
    )
    row_steps = sorted(
        ((co, k) for co in range(1, ncol) for k in range(pieces)),
        key=lambda b: (b[0].bit_length(), b[1], b[0]),
    )
    order = sorted(
        [((i + 1) / len(weights), 0, b) for i, b in enumerate(weights)]
        + [((i + 1) / max(1, len(row_steps)), 1, b) for i, b in enumerate(row_steps)]
    )
    for _, kind, block in order:
        if kind == 0:
            weight_copy(*block).wait_recv()
            have_weight(*block)
        else:
            row_copy(n_ref, n_out, n_send, n_recv, *block).wait_recv()
            gcopy = row_copy(g_ref, g_out, g_send, g_recv, *block)

            @pl.when(decoder)
            def _():
                gcopy.wait_recv()

            have_row(*block)

    for copy in own:
        copy.wait()
    for copy in sent:
        copy.wait_send()
    for copy in gsent:
        @pl.when(decoder)
        def _():
            copy.wait_send()


def gather(split, weights, normed, grads):
    ncol, depth, wide = weights.shape
    rows, width = normed.shape
    pieces = 2
    hbm = pl.BlockSpec(memory_space=pl.ANY)
    dma = pltpu.SemaphoreType.DMA
    return pl.pallas_call(
        functools.partial(gather_kernel, split, pieces),
        out_shape=(
            jax.ShapeDtypeStruct((width, wide), weights.dtype),
            jax.ShapeDtypeStruct((ncol * rows, width), normed.dtype),
            jax.ShapeDtypeStruct((ncol * rows, width), grads.dtype),
        ),
        in_specs=[hbm] * 3,
        out_specs=(hbm,) * 3,
        scratch_shapes=[
            dma((ncol, split.nrow)), dma((ncol, split.nrow)),
            dma((ncol, pieces)), dma((ncol, pieces)),
            dma((ncol, pieces)), dma((ncol, pieces)),
            dma((3,)),
        ],
        compiler_params=pltpu.CompilerParams(collective_id=0, has_side_effects=True),
        name="gather",
    )(weights, normed, grads)


def scatter_kernel(split, p_ref, o_ref, land, held, send, recv, out_send, out_recv, own_sem):
    me = lax.axis_index("dp")
    ncol = split.ncol
    depth = o_ref.shape[1]
    stages = list(reversed(range(len(split.row))))
    my_col = split.col_index(me)
    strip = 64

    def slot(co, ro):
        block = flipped(flipped(me, split.col_mask(co)), split.row_mask(ro))
        return pl.multiple_of(block * depth, depth)

    def copy_of(co, ro):
        stage = ro.bit_length() - 1
        kept = ro - (1 << stage)
        first = stage == stages[0]
        src = p_ref.at[pl.ds(slot(co, ro), depth)] if first else held.at[co, ro]
        return pltpu.make_async_remote_copy(
            src_ref=src, dst_ref=land.at[co, ro], send_sem=send.at[co, ro], recv_sem=recv.at[co, ro],
            device_id={"dp": flipped(me, [split.row[stage]])}, device_id_type=MESH,
        )

    def out_copy(co):
        src = held.at[co, 0]
        return pltpu.make_async_remote_copy(
            src_ref=src, dst_ref=o_ref.at[my_col], send_sem=out_send.at[co], recv_sem=out_recv.at[co],
            device_id={"dp": flipped(me, split.col_mask(co))}, device_id_type=MESH,
        )

    greet(me, split)
    copies = []
    top = 1 << stages[0]
    order = list(reversed(range(ncol)))
    for ro in reversed(range(top)):
        for co in order:
            copy = copy_of(co, top + ro)
            copy.start()
            copies.append(copy)
    for stage in stages:
        bit = 1 << stage
        for ro in reversed(range(bit)):
            for co in order:
                copy_of(co, bit + ro).wait_recv()
                base = slot(co, ro)
                first = stage == stages[0]

                @pl.loop(0, depth // strip)
                def _(i):
                    at = pl.ds(pl.multiple_of(i * strip, strip), strip)
                    if first:
                        mine = p_ref[pl.ds(pl.multiple_of(base + i * strip, strip), strip)]
                    else:
                        mine = held[co, ro, at]
                    other = land[co, bit + ro, at]
                    held[co, ro, at] = (
                        mine.astype(jnp.float32) + other.astype(jnp.float32)
                    ).astype(jnp.bfloat16)

                if ro and ro.bit_length() == stage:
                    copy = copy_of(co, ro)
                    copy.start()
                    copies.append(copy)
                elif ro == 0 and stage == 0:
                    if co:
                        copy = out_copy(co)
                        copy.start()
                        copies.append(copy)
                    else:
                        own = pltpu.make_async_copy(held.at[0, 0], o_ref.at[my_col], own_sem)
                        own.start()
    for co in range(1, ncol):
        out_copy(co).wait_recv()
    own.wait()
    for copy in copies:
        copy.wait_send()


def scatter(split, part, depth):
    ncol, nrow = split.ncol, split.nrow
    wide = part.shape[1]
    dma = pltpu.SemaphoreType.DMA
    vmem = pl.BlockSpec(memory_space=pltpu.VMEM)
    return pl.pallas_call(
        functools.partial(scatter_kernel, split),
        out_shape=jax.ShapeDtypeStruct((ncol, depth, wide), part.dtype),
        in_specs=[vmem],
        out_specs=vmem,
        scratch_shapes=[
            pltpu.VMEM((ncol, nrow, depth, wide), part.dtype),
            pltpu.VMEM((ncol, nrow // 2, depth, wide), part.dtype),
            dma((ncol, nrow)), dma((ncol, nrow)), dma((ncol,)), dma((ncol,)), dma,
        ],
        compiler_params=pltpu.CompilerParams(
            collective_id=1, has_side_effects=True, vmem_limit_bytes=48 * 1024 * 1024
        ),
        name="scatter",
    )(part)


def shards(split, states, loss_grad, gains, w_param, w_fixed, probes):
    ncol, nrow = split.ncol, split.nrow
    is_encoder = lax.axis_index("grp") == 0
    seqs_own, length, width = states.shape[1:]
    rows_own = seqs_own * length
    depth = w_param.shape[1]
    cols_mp = w_param.shape[2]
    cols = cols_mp // ncol
    probe_count = probes.shape[2]
    heads = cols // HEAD
    rows = rows_own * ncol
    seqs = seqs_own * ncol

    normed_own = normalize(states[0].reshape(rows_own, width), gains[0])
    grads_own = loss_grad.reshape(rows_own, width)

    wcat = jnp.concatenate([w_param[0][:, None], probes[0], w_fixed[0][:, None]], axis=1)
    wcat = wcat.reshape(depth, 2 + probe_count, ncol, cols)
    wcat = jnp.transpose(wcat, (2, 0, 1, 3)).reshape(ncol, depth, (2 + probe_count) * cols)
    w_all, normed, grads = gather(split, wcat, normed_own, grads_own)
    source = jnp.where(is_encoder, normed, grads)

    wide = (1 + probe_count) * cols
    first = jnp.dot(normed, w_all[:, :wide], preferred_element_type=jnp.float32).astype(jnp.bfloat16)
    second = jnp.dot(source, w_all[:, wide:], preferred_element_type=jnp.float32).astype(jnp.bfloat16)

    k_first, k_second = passed_along((first, second), "grp", 1)

    def heads_of(x):
        return x.astype(jnp.float32).reshape(seqs, length, heads, HEAD)

    def probe_heads(x):
        return jnp.moveaxis(
            x.astype(jnp.float32).reshape(seqs, length, probe_count, heads, HEAD), 2, 0
        )

    def back_rows(x):
        return jnp.moveaxis(x, 0, 2).reshape(rows, probe_count * cols).astype(jnp.bfloat16)

    weight = float(rows_own * ncol * nrow) ** (-0.5)
    d_query, d_keys = curvature(
        heads_of(first[:, :cols]),
        heads_of(k_first[:, :cols]),
        heads_of(k_second),
        heads_of(second),
        probe_heads(first[:, cols:]),
        probe_heads(k_first[:, cols:]),
        weight,
    )
    d_query = back_rows(d_query)
    d_keys = back_rows(d_keys)
    returned = passed_along(d_keys, "grp", -1)
    chosen = jnp.where(is_encoder, returned, d_query)
    part = lax.dot_general(
        normed, chosen, (((0,), (0,)), ((), ())), preferred_element_type=jnp.float32
    ).astype(jnp.bfloat16)
    out = scatter(split, part, depth)
    out = jnp.transpose(out.reshape(ncol, depth, probe_count, cols), (1, 2, 0, 3))
    return out.reshape(1, depth, probe_count, cols_mp)


def solution(mesh):
    dp, mp = (mesh.shape[name] for name in ("dp", "mp"))
    in_specs = (
        P("grp", "dp", None, None),
        P("dp", None, None),
        P("grp", None),
        P("grp", "dp", "mp"),
        P("grp", "dp", "mp"),
        P("grp", "dp", None, "mp"),
    )
    out_specs = P("grp", "dp", None, "mp")

    def run(states, loss_grad, gains, w_param, w_fixed, probes):
        split = Split(dp, w_param.shape[2] // mp // HEAD)
        return jax.shard_map(
            functools.partial(shards, split),
            mesh=mesh, in_specs=in_specs, out_specs=out_specs, check_vma=False,
        )(states, loss_grad, gains, w_param, w_fixed, probes)

    return run
```

time: 821 us -> 574 us (0.70)
  Pallas kernels: 0 us -> 394 us
  waiting for transfers between devices: 379 us -> 0.01 us
  blocking collectives: 262 us -> 0 us
  starting transfers between devices: 7.93 us -> 26.8 us
  between operations: 13.5 us -> 0.3 us
    pallas_call x0 -> x2, Pallas kernels: none -> 394 us  [the longest x1 261 us: gather(): pl.pallas_call(functools.partial(gather_kernel, split, pieces), out_shape...]
    all_gather x3 -> x0, waiting for transfers between devices: 292 us -> none  [the longest x1 159 us: shards(): w_all = lax.all_gather(mine, 'r', axis=0, tiled=True)]
    all_to_all x2 -> x0, blocking collectives: 262 us -> none  [the longest x1 210 us: shards(): mine = lax.all_to_all(wcat, 'c', split_axis=0, concat_axis=0, tiled=True)]
    reduce_scatter x1 -> x0, waiting for transfers between devices: 86.4 us -> none  [shards(): summed = lax.psum_scatter(part, 'r', scatter_dimension=0, tiled=True)]
    ppermute x3, starting transfers between devices: 7.81 us -> 26.8 us  [passed_along(): lax.ppermute(value, axis, [(source, source + steps) for source in range(f...]
    concatenate x0 -> x6, local copies, waits for them, and re-layouts: none -> 14.9 us  [shards(): jnp.concatenate([w_param[0][:, None], probes[0], w_fixed[0][:, None]], ax...]
    unnamed x43 -> x35, local copies, waits for them, and re-layouts: 17.4 us -> 7.74 us
  transfers between devices with their start and end apart: 7 -> 3, of which waited for: 4 -> 0; matrix products, arithmetic and copies ran while one was open for 10% -> 6% of each run, Pallas kernels for 0% -> 0%
where the time goes in v2:
time: 574 us; the launch traced here: 573 us
  Pallas kernels  394 us (69%)
  local copies, waits for them, and re-layouts  72.2 us (13%)
  matrix products  65 us (11%)
  starting transfers between devices  26.8 us (5%)
  other arithmetic  14.4 us (3%)
    pallas_call x1, Pallas kernels, gather(): pl.pallas_call(functools.partial(gather_kernel, split, pieces), out_shape...  261 us
    pallas_call x1, Pallas kernels, scatter(): pl.pallas_call(functools.partial(scatter_kernel, split), out_shape=jax.Sh...  133 us
    ppermute x3, starting transfers between devices, passed_along(): lax.ppermute(value, axis, [(source, source + steps) for source in range(f...  26.8 us
    dot_general x7, matrix products, attention_loss(): scores = jnp.einsum('sihe,sjhe->shij', query, keys)  19.6 us
    dot_general x1, matrix products, shards(): jnp.dot(normed, w_all[:, :wide], preferred_element_type=jnp.float32)  19.4 us
    dot_general x1, matrix products, shards(): lax.dot_general(normed, chosen, (((0,), (0,)), ((), ())), preferred_eleme...  15.4 us
    concatenate x6, local copies, waits for them, and re-layouts, shards(): jnp.concatenate([w_param[0][:, None], probes[0], w_fixed[0][:, None]], ax...  14.9 us
  transfers between devices with their start and end apart: 3, of which 0 were waited for; matrix products, arithmetic and copies ran while one was open for 6% of the time, Pallas kernels for 0%

profile of v2, /device:TPU:0, one launch (start us, length us, event | category | flops | bytes accessed | tf_op | source)
XLA Modules:
  0.0 572.6 jit_solution(4860419552051082823)
XLA Ops:
  0.0 2.2 multiply_reduce_fusion
  4.6 1.8 concatenate.12
  6.5 2.9 copy.25
  9.4 4.4 concatenate.11
  13.8 3.4 copy.24
  17.1 8.1 %maximum_bitcast_fusion = bf16[4,256,4,512]{3,2,1,0:T(4,128)(2,1)} fusion(bf16[256,1,4,512]{3,1,0,2:T(2,128)(2,1)S(1)} %copy-done.10, bf16[256,2,4,512]{3,1,0,2:T(2,128)(2,1)S(1)} %copy.24, bf16[256,1,4,512]{3,1,0,2:T(2,128)(2,1)S(1)} %copy.23), kind=kLoop, calls=%fused_computation.6 | loop fusion | flops 12582912 | bytes 8388608 | tf_op jit(solution)/shard_map/transpose | solution.py:359
  25.2 7.9 %reshape.103.w_ref = bf16[4,256,2048]{2,1,0:T(8,128)(2,1)} reshape(bf16[4,256,4,512]{3,2,1,0:T(4,128)(2,1)} %maximum_bitcast_fusion) | data formatting | bytes 8388608 | tf_op jit(solution)/shard_map/reshape | solution.py:359
  33.1 1.9 fusion.8.n_ref
  35.1 261.2 %gather.1 = (bf16[4096,2048]{1,0:T(8,128)(2,1)}, bf16[1024,4096]{1,0:T(8,128)(2,1)}, bf16[1024,4096]{1,0:T(8,128)(2,1)}) custom-call(bf16[4,256,2048]{2,1,0:T(8,128)(2,1)} %reshape.103.w_ref, bf16[256,4096]{1,0:T(8,128)(2,1)} %fusion.8.n_ref, bf16[256,4096]{1,0:T(8,128)(2,1)} %bitcast.85), custom_call_target="tpu_custom_call" | custom-call | tf_op jit(solution)/shard_map/gather/pallas_call | solution.py:222
  296.3 19.4 %fusion.10 = bf16[1024,1536]{1,0:T(8,128)(2,1)} fusion(bf16[1024,4096]{1,0:T(8,128)(2,1)} %get-tuple-element.8, bf16[4096,2048]{1,0:T(8,128)(2,1)} %get-tuple-element.9), kind=kOutput, calls=%fused_computation.16 | convolution fusion | flops 12886474752 | bytes 24117248 | tf_op jit(solution)/shard_map/dot_general | solution.py:364
  315.7 23.2 %collective-permute-start = (bf16[1024,1536]{1,0:T(8,128)(2,1)}, bf16[1024,1536]{1,0:T(8,128)(2,1)}, u32[]{:S(2)}, u32[]{:S(2)}) collective-permute-start(bf16[1024,1536]{1,0:T(8,128)(2,1)} %fusion.10), channel_id=1, source_target_pairs={{0,16},{1,17},{2,18},{3,19},{4,20},{5,21},{6,22},{7,23},{8,24},{9,... | collective-permute-start | bytes 9437192 | tf_op jit(solution)/shard_map/ppermute | solution.py:26
  338.9 10.1 %fusion.28 = bf16[1024,512]{1,0:T(8,128)(2,1)} fusion(bf16[4096,2048]{1,0:T(8,128)(2,1)} %get-tuple-element.9, bf16[1024,4096]{1,0:T(8,128)(2,1)} %get-tuple-element.8, bf16[1024,4096]{1,0:T(8,128)(2,1)} %get-tuple-element.10, pred[]{:T(512)S(6)} %eq.3), kind=kOutput, calls=%fused_computation.35 | convolution fusion | flops 4299685888 | bytes 22020096 | tf_op jit(solution)/shard_map/dot_general | solution.py:365
  349.0 2.3 collective-permute-start.1
  352.6 2.4 reshape.109
  355.0 3.1 slice.24
  359.2 3.3 reshape.105
  362.5 2.9 reshape.110
  365.4 3.1 slice.27
  368.5 4.5 reshape.108
  373.0 2.3 slice.25
  386.8 2.8 fusion.34
  389.6 5.9 %fusion.6 = bf16[8,128,2,2,256]{4,1,2,3,0:T(8,128)(2,1)} fusion(f32[8,2,2,128,256]{4,3,2,1,0:T(8,128)} %fusion.34, bf16[8,128,2,2,256]{4,3,2,1,0:T(2,128)(2,1)} %copy-done.2, f32[8,2,128,128]{2,3,1,0:T(8,128)} %copy-done, f32[8,2,128,128]{2,3,1,0:T(8,128)} %copy-done.12), kind=kOutput, calls=%fused_computation.10 | convolution fusion | flops 271059072 | bytes 10485760 | tf_op jit(solution)/shard_map/vmap(jvp(transpose(jvp(sihe,sjhe->shij))))/dot_general | solution.py:30
  395.5 4.3 copy.35
  399.8 3.7 copy.107
  404.8 2.9 fusion.33
  407.8 4.6 fusion.5
  412.4 2.9 copy.39
  415.2 15.4 %convolution_convert_fusion.p_ref = bf16[4096,1024]{1,0:T(8,128)(2,1)} fusion(bf16[1024,4096]{1,0:T(8,128)(2,1)} %get-tuple-element.8, bf16[1024,1024]{0,1:T(8,128)(2,1)} %collective-permute-done.2, bf16[128,8,8,128]{3,2,1,0:T(8,128)(2,1)} %bitcast.84, pred[]{:T(512)S(6)} %eq.3), kind=kOutput, calls=%fused_computation.5 | convolution fusion | flops 8595177472 | bytes 20971520 | tf_op jit(solution)/shard_map/dot_general | solution.py:394
  430.6 132.8 %scatter.1 = bf16[4,256,1024]{2,1,0:T(8,128)(2,1)S(1)} custom-call(bf16[4096,1024]{1,0:T(8,128)(2,1)} %convolution_convert_fusion.p_ref), custom_call_target="tpu_custom_call" | custom-call | tf_op jit(solution)/shard_map/scatter/pallas_call | solution.py:324
  563.4 2.8 reshape.111
  566.1 4.3 copy.40
  570.4 2.2 reshape.112
  (55 shorter events, 17.5 us)
Async XLA Ops:
  0.0 2.2 copy-start.15
  13.8 3.4 copy-start.10
  25.2 7.9 %copy-start.11 = (bf16[1,2,128,4096]{3,2,1,0:T(8,128)(2,1)S(1)}, bf16[1,2,128,4096]{3,2,1,0:T(8,128)(2,1)}, u32[]{:S(2)}) copy-start(bf16[1,2,128,4096]{3,2,1,0:T(8,128)(2,1)} %param.6) | copy-start | bytes 6291460
  25.2 7.9 %copy-start.16 = (f32[1,4096]{1,0:T(1,128)S(1)}, f32[1,4096]{1,0:T(1,128)}, u32[]{:S(2)}) copy-start(f32[1,4096]{1,0:T(1,128)} %param.8) | copy-start | bytes 49156
  315.7 49.7 %collective-permute-start = (bf16[1024,1536]{1,0:T(8,128)(2,1)}, bf16[1024,1536]{1,0:T(8,128)(2,1)}, u32[]{:S(2)}, u32[]{:S(2)}) collective-permute-start(bf16[1024,1536]{1,0:T(8,128)(2,1)} %fusion.10), channel_id=1, source_target_pairs={{0,16},{1,17},{2,18},{3,19},{4,20},{5,21},{6,22},{7,23},{8,24},{9,... | collective-permute-start | bytes 9437192 | tf_op jit(solution)/shard_map/ppermute | solution.py:26
  349.0 13.5 %collective-permute-start.1 = (bf16[1024,512]{1,0:T(8,128)(2,1)}, bf16[1024,512]{1,0:T(8,128)(2,1)}, u32[]{:S(2)}, u32[]{:S(2)}) collective-permute-start(bf16[1024,512]{1,0:T(8,128)(2,1)} %fusion.28), channel_id=1, source_target_pairs={{0,16},{1,17},{2,18},{3,19},{4,20},{5,21},{6,22},{7,23},{8,24},{9,... | collective-permute-start | bytes 3145736 | tf_op jit(solution)/shard_map/ppermute | solution.py:26
  362.5 19.8 %copy-start.2 = (bf16[8,128,2,2,256]{4,3,2,1,0:T(2,128)(2,1)}, bf16[8,128,2,2,256]{4,3,2,1,0:T(2,128)(2,1)S(1)}, u32[]{:S(2)}) copy-start(bf16[8,128,2,2,256]{4,3,2,1,0:T(2,128)(2,1)S(1)} %reshape.105) | copy-start | bytes 6291460
  376.6 1.0 copy-start.6
  377.6 3.8 copy-start.13
  377.6 3.8 copy-start.14
  379.4 1.0 copy-start.12
  382.0 1.3 copy-start.7
  382.2 4.5 copy-start
  382.2 4.5 copy-start.4
  383.3 1.6 copy-start.3
  383.3 1.9 copy-start.9
  399.8 5.0 copy-start.1
  399.8 5.0 copy-start.5
  399.8 5.0 copy-start.8
  403.5 11.7 %collective-permute-start.2 = (bf16[1024,1024]{0,1:T(8,128)(2,1)}, bf16[1024,1024]{0,1:T(8,128)(2,1)}, u32[]{:S(2)}, u32[]{:S(2)}) collective-permute-start(bf16[1024,1024]{0,1:T(8,128)(2,1)} %bitcast.77), channel_id=1, source_target_pairs={{16,0},{17,1},{18,2},{19,3},{20,4},{21,5},{22,6},{23,7},{24,8},{25... | collective-permute-start | bytes 6291464 | tf_op jit(solution)/shard_map/ppermute | solution.py:26

commit v3 on v2

--- a/solution.py
+++ b/solution.py
@@ -20,28 +20,65 @@
     return (values * scale * gain).astype(jnp.bfloat16)
 
 
-def passed_along(value, axis, steps):
-    count = lax.axis_size(axis)
-    first, last = (max(0, -steps), min(count, count - steps))
-    return lax.ppermute(value, axis, [(source, source + steps) for source in range(first, last)])
-
-
-def attention_loss(query, keys, values, out_grad, weight):
-    scores = jnp.einsum("sihe,sjhe->shij", query, keys)
-    probs = jax.nn.softmax(scores, axis=-1)
-    mixing = jnp.einsum("sihe,sjhe->shij", out_grad, values)
-    return jnp.sum(probs * mixing) * weight
-
-
-def curvature(query, keys, values, out_grad, t_query, t_keys, weight):
-
-    def grads(q_arg, k_arg):
-        return jax.grad(attention_loss, argnums=(0, 1))(q_arg, k_arg, values, out_grad, weight)
-
-    def along(a_dir, b_dir):
-        return jax.jvp(grads, (query, keys), (a_dir, b_dir))[1]
-
-    return jax.vmap(along)(t_query, t_keys)
+def swapped(value):
+    return lax.ppermute(value, "grp", [(0, 1), (1, 0)])
+
+
+def attention_kernel(heads, probe_count, weight, keep, keep_last, other, other_last, own, theirs):
+    encoder = lax.axis_index("grp") == 0
+    cols = heads * HEAD
+
+    def dot(a, b, dims):
+        return lax.dot_general(a, b, ((dims[0], dims[1]), ((), ())), preferred_element_type=jnp.float32)
+
+    nt, nn, tn = ((1,), (1,)), ((1,), (0,)), ((0,), (0,))
+
+    def sides(mine, yours, at):
+        x, y = mine[:, at : at + HEAD], yours[:, at : at + HEAD]
+        return jnp.where(encoder, x, y), jnp.where(encoder, y, x)
+
+    for h in range(heads):
+        at = h * HEAD
+        k, q = sides(keep, other, at)
+        v, o = sides(keep_last, other_last, at)
+        scores = dot(q, k, nt)
+        top = jnp.exp(scores - jnp.max(scores, axis=-1, keepdims=True))
+        probs = top / jnp.sum(top, axis=-1, keepdims=True)
+        mixing = dot(o, v, nt)
+        centred = mixing - jnp.sum(probs * mixing, axis=-1, keepdims=True)
+        grad = (probs * centred * weight).astype(jnp.bfloat16)
+        for p in range(probe_count):
+            pat = (1 + p) * cols + at
+            tk, tq = sides(keep, other, pat)
+            d_scores = dot(tq, k, nt) + dot(q, tk, nt)
+            d_probs = probs * (d_scores - jnp.sum(probs * d_scores, axis=-1, keepdims=True))
+            d_mean = jnp.sum(d_probs * mixing, axis=-1, keepdims=True)
+            d_grad = ((d_probs * centred - probs * d_mean) * weight).astype(jnp.bfloat16)
+            dq = (dot(d_grad, k, nn) + dot(grad, tk, nn)).astype(jnp.bfloat16)
+            dk = (dot(d_grad, q, tn) + dot(grad, tq, tn)).astype(jnp.bfloat16)
+            out = p * cols + at
+            own[:, out : out + HEAD] = jnp.where(encoder, dk, dq)
+            theirs[:, out : out + HEAD] = jnp.where(encoder, dq, dk)
+
+
+def attention(keep, keep_last, other, other_last, length, probe_count, weight):
+    rows, cols = keep_last.shape
+    heads = cols // HEAD
+
+    def block(width):
+        return pl.BlockSpec((length, width), lambda s: (s, 0))
+
+    wide, out = keep.shape[1], probe_count * cols
+    shape = jax.ShapeDtypeStruct((rows, out), jnp.bfloat16)
+    return pl.pallas_call(
+        functools.partial(attention_kernel, heads, probe_count, weight),
+        grid=(rows // length,),
+        out_shape=(shape, shape),
+        in_specs=[block(wide), block(cols), block(wide), block(cols)],
+        out_specs=(block(out), block(out)),
+        compiler_params=pltpu.CompilerParams(vmem_limit_bytes=32 * 1024 * 1024),
+        name="attention",
+    )(keep, keep_last, other, other_last)
 
 
 class Split:
@@ -87,11 +124,15 @@
                   w_send, w_recv, n_send, n_recv, g_send, g_recv, own_sem):
     me = lax.axis_index("dp")
     decoder = lax.axis_index("grp") != 0
-    depth = w_ref.shape[1]
     ncol, nrow = split.ncol, split.nrow
+    depth = w_ref.shape[0]
+    wide = w_ref.shape[1] // ncol
     my_col = split.col_index(me)
     rows = n_ref.shape[0]
     piece = rows // pieces
+
+    def weight_own(col):
+        return w_ref.at[:, pl.ds(pl.multiple_of(col * wide, wide), wide)]
 
     def weight_slot(cs, ro):
         source = flipped(flipped(me, split.col_mask(cs)), split.row_mask(ro))
@@ -115,11 +156,11 @@
     def weight_copy(cs, ro):
         if ro == 0:
             dest = split.col_index(flipped(me, split.col_mask(cs)))
-            return remote(w_ref.at[dest], weight_slot(0, 0), w_send.at[cs, 0], w_recv.at[cs, 0],
+            return remote(weight_own(dest), weight_slot(0, 0), w_send.at[cs, 0], w_recv.at[cs, 0],
                           split.col_mask(cs))
         stage = ro.bit_length() - 1
         held = ro - (1 << stage)
-        src = w_ref.at[my_col] if (cs, held) == (0, 0) else weight_slot(cs, held)
+        src = weight_own(my_col) if (cs, held) == (0, 0) else weight_slot(cs, held)
         return remote(src, weight_slot(cs, held), w_send.at[cs, ro], w_recv.at[cs, ro],
                       [split.row[stage]])
 
@@ -166,7 +207,7 @@
         have_row(0, k)
 
     own = [
-        pltpu.make_async_copy(w_ref.at[my_col], weight_slot(0, 0), own_sem.at[0]),
+        pltpu.make_async_copy(weight_own(my_col), weight_slot(0, 0), own_sem.at[0]),
         pltpu.make_async_copy(
             n_ref, n_out.at[pl.ds(pl.multiple_of(my_col * rows, rows), rows)], own_sem.at[1]
         ),
@@ -214,7 +255,7 @@
 
 
 def gather(split, weights, normed, grads):
-    ncol, depth, wide = weights.shape
+    ncol, wide = split.ncol, weights.shape[1] // split.ncol
     rows, width = normed.shape
     pieces = 2
     hbm = pl.BlockSpec(memory_space=pl.ANY)
@@ -347,16 +388,15 @@
     cols_mp = w_param.shape[2]
     cols = cols_mp // ncol
     probe_count = probes.shape[2]
-    heads = cols // HEAD
     rows = rows_own * ncol
-    seqs = seqs_own * ncol
 
     normed_own = normalize(states[0].reshape(rows_own, width), gains[0])
     grads_own = loss_grad.reshape(rows_own, width)
 
-    wcat = jnp.concatenate([w_param[0][:, None], probes[0], w_fixed[0][:, None]], axis=1)
-    wcat = wcat.reshape(depth, 2 + probe_count, ncol, cols)
-    wcat = jnp.transpose(wcat, (2, 0, 1, 3)).reshape(ncol, depth, (2 + probe_count) * cols)
+    units = [w_param[0], *(probes[0, :, p] for p in range(probe_count)), w_fixed[0]]
+    wcat = jnp.concatenate(
+        [unit[:, c * cols : (c + 1) * cols] for c in range(ncol) for unit in units], axis=1
+    )
     w_all, normed, grads = gather(split, wcat, normed_own, grads_own)
     source = jnp.where(is_encoder, normed, grads)
 
@@ -364,33 +404,21 @@
     first = jnp.dot(normed, w_all[:, :wide], preferred_element_type=jnp.float32).astype(jnp.bfloat16)
     second = jnp.dot(source, w_all[:, wide:], preferred_element_type=jnp.float32).astype(jnp.bfloat16)
 
-    k_first, k_second = passed_along((first, second), "grp", 1)
-
-    def heads_of(x):
-        return x.astype(jnp.float32).reshape(seqs, length, heads, HEAD)
-
-    def probe_heads(x):
-        return jnp.moveaxis(
-            x.astype(jnp.float32).reshape(seqs, length, probe_count, heads, HEAD), 2, 0
-        )
-
-    def back_rows(x):
-        return jnp.moveaxis(x, 0, 2).reshape(rows, probe_count * cols).astype(jnp.bfloat16)
-
+    half = rows // 2
+    grp = lax.axis_index("grp")
+
+    def halves(x):
+        keep = lax.dynamic_slice_in_dim(x, grp * half, half, 0)
+        return keep, swapped(lax.dynamic_slice_in_dim(x, (1 - grp) * half, half, 0))
+
+    keep, other = halves(first)
+    keep_last, other_last = halves(second)
     weight = float(rows_own * ncol * nrow) ** (-0.5)
-    d_query, d_keys = curvature(
-        heads_of(first[:, :cols]),
-        heads_of(k_first[:, :cols]),
-        heads_of(k_second),
-        heads_of(second),
-        probe_heads(first[:, cols:]),
-        probe_heads(k_first[:, cols:]),
-        weight,
-    )
-    d_query = back_rows(d_query)
-    d_keys = back_rows(d_keys)
-    returned = passed_along(d_keys, "grp", -1)
-    chosen = jnp.where(is_encoder, returned, d_query)
+    own, theirs = attention(keep, keep_last, other, other_last, length, probe_count, weight)
+    back = swapped(theirs)
+    chosen = jnp.concatenate(
+        [jnp.where(is_encoder, own, back), jnp.where(is_encoder, back, own)], axis=0
+    )
     part = lax.dot_general(
         normed, chosen, (((0,), (0,)), ((), ())), preferred_element_type=jnp.float32
     ).astype(jnp.bfloat16)

time: 574 us -> 500 us (0.87)
  local copies, waits for them, and re-layouts: 72.2 us -> 29.8 us
  matrix products: 65 us -> 42.1 us
  other arithmetic: 14.4 us -> 2.6 us
  Pallas kernels: 394 us -> 401 us
  starting transfers between devices: 26.8 us -> 20 us
    reshape x7 -> x0, local copies, waits for them, and re-layouts: 23.4 us -> none  [the longest x1 7.9 us: shards(): jnp.transpose(wcat, (2, 0, 1, 3))]
    dot_general x8 -> x0, matrix products: 20.1 us -> none  [the longest x7 19.6 us: attention_loss(): scores = jnp.einsum('sihe,sjhe->shij', query, keys)]
    concatenate x6 -> x1, local copies, waits for them, and re-layouts: 14.9 us -> 0.76 us  [shards(): jnp.concatenate([unit[:, c * cols:(c + 1) * cols] for c in range(ncol) fo...]
    transpose x1 -> x0, other arithmetic: 8.09 us -> none  [shards(): jnp.transpose(wcat, (2, 0, 1, 3))]
    pallas_call x0 -> x1, Pallas kernels: none -> 7.6 us  [attention(): pl.pallas_call(functools.partial(attention_kernel, heads, probe_count, we...]
    convert_element_type x2 -> x0, local copies, waits for them, and re-layouts: 7.13 us -> none  [back_rows(): jnp.moveaxis(x, 0, 2).reshape(rows, probe_count * cols).astype(jnp.bfloat16)]
    ppermute x3, starting transfers between devices: 26.8 us -> 20 us  [swapped(): return lax.ppermute(value, 'grp', [(0, 1), (1, 0)])]
  transfers between devices with their start and end apart: 3 -> 3, of which waited for: 0 -> 2; matrix products, arithmetic and copies ran while one was open for 6% -> 2% of each run, Pallas kernels for 0% -> 0%
where the time goes in v3:
time: 500 us
  Pallas kernels  401 us (80%)
  matrix products  42.1 us (8%)
  local copies, waits for them, and re-layouts  29.8 us (6%)
  starting transfers between devices  20 us (4%)
    pallas_call x1, Pallas kernels, gather(): pl.pallas_call(functools.partial(gather_kernel, split, pieces), out_shape...  261 us
    pallas_call x1, Pallas kernels, scatter(): pl.pallas_call(functools.partial(scatter_kernel, split), out_shape=jax.Sh...  132 us
    ppermute x3, starting transfers between devices, swapped(): return lax.ppermute(value, 'grp', [(0, 1), (1, 0)])  20 us
    dot_general x1, matrix products, shards(): jnp.dot(normed, w_all[:, :wide], preferred_element_type=jnp.float32)  18.2 us
    dot_general x1, matrix products, shards(): lax.dot_general(normed, chosen, (((0,), (0,)), ((), ())), preferred_eleme...  14.8 us
    unnamed x23, local copies, waits for them, and re-layouts  11.4 us
  transfers between devices with their start and end apart: 3, of which 2 were waited for; matrix products, arithmetic and copies ran while one was open for 2% of the time, Pallas kernels for 0%

profile of v3, /device:TPU:0, one launch (start us, length us, event | category | flops | bytes accessed | tf_op | source)
XLA Modules:
  0.0 499.6 jit_solution(3377130066424825422)
XLA Ops:
  0.0 5.6 %fusion.20 = (bf16[1,256,1,2048]{3,2,1,0:T(2,128)(2,1)S(1)}, bf16[1,256,1,2048]{3,2,1,0:T(2,128)(2,1)S(1)}) fusion(bf16[1,256,2,2048]{3,2,1,0:T(2,128)(2,1)} %param.11), kind=kLoop, calls=%fused_computation.42 | loop fusion | bytes 4194304 | tf_op jit(solution)/shard_map/slice | solution.py:396
  5.7 0.7 slice_dynamic-update-slice_fusion.15
  6.4 1.3 copy_bitcast_fusion
  7.7 0.7 slice_dynamic-update-slice_fusion.14
  8.5 0.8 slice_dynamic-update-slice_fusion.13
  9.2 0.8 slice_dynamic-update-slice_fusion.12
  10.0 0.7 slice_dynamic-update-slice_fusion.11
  10.7 0.8 slice_dynamic-update-slice_fusion.10
  11.5 0.8 slice_dynamic-update-slice_fusion.9
  12.2 0.7 slice_dynamic-update-slice_fusion.8
  13.0 0.8 slice_dynamic-update-slice_fusion.7
  13.8 0.8 slice_dynamic-update-slice_fusion.6
  14.6 0.8 slice_dynamic-update-slice_fusion.5
  15.4 0.8 slice_dynamic-update-slice_fusion.4
  16.1 0.8 slice_dynamic-update-slice_fusion.3
  16.9 0.7 slice_dynamic-update-slice_fusion.2
  17.6 0.7 slice_dynamic-update-slice_fusion.1
  18.4 0.8 slice_dynamic-update-slice_fusion.w_ref
  19.7 2.0 fusion.6.n_ref
  21.6 261.2 %gather.1 = (bf16[4096,2048]{1,0:T(8,128)(2,1)}, bf16[1024,4096]{1,0:T(8,128)(2,1)}, bf16[1024,4096]{1,0:T(8,128)(2,1)}) custom-call(bf16[256,8192]{1,0:T(8,128)(2,1)} %slice_dynamic-update-slice_fusion.w_ref, bf16[256,4096]{1,0:T(8,128)(2,1)} %fusion.6.n_ref, bf16[256,4096]{1,0:T(8,128)(2,1)} %bitcast.20), custom_call_target="tpu_custom_call" | custom-call | tf_op jit(solution)/shard_map/gather/pallas_call | solution.py:263
  282.8 18.2 %fusion.8 = bf16[1024,1536]{1,0:T(8,128)(2,1)S(1)} fusion(bf16[1024,4096]{1,0:T(8,128)(2,1)} %get-tuple-element.10, bf16[4096,2048]{1,0:T(8,128)(2,1)} %get-tuple-element.11), kind=kOutput, calls=%fused_computation.11 | convolution fusion | flops 12886474752 | bytes 24117248 | tf_op jit(solution)/shard_map/dot_general | solution.py:404
  301.0 1.4 constant_dynamic-slice_fusion.1
  302.4 19.7 %collective-permute-start = (bf16[512,1536]{1,0:T(8,128)(2,1)}, bf16[512,1536]{1,0:T(8,128)(2,1)S(1)}, u32[]{:S(2)}, u32[]{:S(2)}) collective-permute-start(bf16[512,1536]{1,0:T(8,128)(2,1)} %get-tuple-element.15), channel_id=1, source_target_pairs={{0,16},{16,0},{1,17},{17,1},{2,18},{18,2},{3,19},{19,3},{4,20},{20... | collective-permute-start | bytes 4718600 | tf_op jit(solution)/shard_map/ppermute | solution.py:24
  322.1 9.1 %fusion.14 = bf16[1024,512]{1,0:T(8,128)(2,1)S(1)} fusion(bf16[4096,2048]{1,0:T(8,128)(2,1)} %get-tuple-element.11, bf16[1024,4096]{1,0:T(8,128)(2,1)} %get-tuple-element.10, bf16[1024,4096]{1,0:T(8,128)(2,1)} %get-tuple-element.12, pred[]{:T(512)S(6)} %eq.3), kind=kOutput, calls=%fused_computation.15 | convolution fusion | flops 4299685888 | bytes 22020096 | tf_op jit(solution)/shard_map/dot_general | solution.py:405
  331.3 1.9 collective-permute-done.1.other_last
  333.2 7.6 %attention.1 = (bf16[512,1024]{1,0:T(8,128)(2,1)S(1)}, bf16[512,1024]{1,0:T(8,128)(2,1)S(1)}) custom-call(bf16[512,1536]{1,0:T(8,128)(2,1)S(1)} %get-tuple-element.16.keep, bf16[512,512]{1,0:T(8,128)(2,1)S(1)} %get-tuple-element.22.keep_last, bf16[512,1536]{1,0:T(8,128)(2,1)S(1)} %collective-permute-done.other, ...), custom_call_target="tpu_custom_call" | custom-call | tf_op jit(solution)/shard_map/attention/pallas_call | solution.py:73
  341.0 2.5 collective-permute-done.2
  343.7 14.8 %convolution_convert_fusion.p_ref = bf16[4096,1024]{1,0:T(8,128)(2,1)} fusion(bf16[1024,4096]{1,0:T(8,128)(2,1)} %get-tuple-element.10, bf16[512,1024]{1,0:T(8,128)(2,1)S(1)} %get-tuple-element.18, bf16[512,1024]{1,0:T(8,128)(2,1)S(1)} %get-tuple-element.17), kind=kOutput, calls=%fused_computation.5 | convolution fusion | flops 8598323200 | bytes 18874368 | tf_op jit(solution)/shard_map/dot_general | solution.py:422
  358.5 131.8 %scatter.1 = bf16[4,256,1024]{2,1,0:T(8,128)(2,1)S(1)} custom-call(bf16[4096,1024]{1,0:T(8,128)(2,1)} %convolution_convert_fusion.p_ref), custom_call_target="tpu_custom_call" | custom-call | tf_op jit(solution)/shard_map/scatter/pallas_call | solution.py:365
  490.3 2.8 reshape.29
  493.1 4.3 copy.9
  497.3 2.2 reshape.30
  (15 shorter events, 1.0 us)
Async XLA Ops:
  0.0 5.7 %copy-start.1 = (bf16[1,256,2048]{2,1,0:T(8,128)(2,1)S(1)}, bf16[1,256,2048]{2,1,0:T(8,128)(2,1)}, u32[]{:S(2)}) copy-start(bf16[1,256,2048]{2,1,0:T(8,128)(2,1)} %param.9) | copy-start | bytes 3145732
  5.7 3.6 copy-start.2
  7.7 11.5 %copy-start = (bf16[1,2,128,4096]{3,2,1,0:T(8,128)(2,1)S(1)}, bf16[1,2,128,4096]{3,2,1,0:T(8,128)(2,1)}, u32[]{:S(2)}) copy-start(bf16[1,2,128,4096]{3,2,1,0:T(8,128)(2,1)} %param.6) | copy-start | bytes 6291460
  10.0 9.7 %copy-start.3 = (f32[1,4096]{1,0:T(1,128)S(1)}, f32[1,4096]{1,0:T(1,128)}, u32[]{:S(2)}) copy-start(f32[1,4096]{1,0:T(1,128)} %param.8) | copy-start | bytes 49156
  302.4 30.8 %collective-permute-start = (bf16[512,1536]{1,0:T(8,128)(2,1)}, bf16[512,1536]{1,0:T(8,128)(2,1)S(1)}, u32[]{:S(2)}, u32[]{:S(2)}) collective-permute-start(bf16[512,1536]{1,0:T(8,128)(2,1)} %get-tuple-element.15), channel_id=1, source_target_pairs={{0,16},{16,0},{1,17},{17,1},{2,18},{18,2},{3,19},{19,3},{4,20},{20... | collective-permute-start | bytes 4718600 | tf_op jit(solution)/shard_map/ppermute | solution.py:24
  331.2 2.0 collective-permute-start.1
  340.8 2.7 collective-permute-start.2

commit v4 on v3

--- a/solution.py
+++ b/solution.py
@@ -203,8 +203,6 @@
     for cs in range(1, ncol):
         start_weight(cs, 0)
     have_weight(0, 0)
-    for k in range(pieces):
-        have_row(0, k)
 
     own = [
         pltpu.make_async_copy(weight_own(my_col), weight_slot(0, 0), own_sem.at[0]),
@@ -218,18 +216,23 @@
     for copy in own:
         copy.start()
 
-    weights = sorted(
-        ((cs, ro) for cs in range(ncol) for ro in range(nrow) if (cs, ro) != (0, 0)),
-        key=lambda b: (b[1].bit_length() + (1 if b[0] else 0), b[1], b[0]),
-    )
-    row_steps = sorted(
-        ((co, k) for co in range(1, ncol) for k in range(pieces)),
-        key=lambda b: (b[0].bit_length(), b[1], b[0]),
-    )
-    order = sorted(
-        [((i + 1) / len(weights), 0, b) for i, b in enumerate(weights)]
-        + [((i + 1) / max(1, len(row_steps)), 1, b) for i, b in enumerate(row_steps)]
-    )
+    for cs in range(1, ncol):
+        weight_copy(cs, 0).wait_recv()
+        have_weight(cs, 0)
+        for stage in range(col_stages):
+            if cs == 1 << stage:
+                for k in range(pieces):
+                    start_row(cs, k)
+
+    weights = [(ro.bit_length() == row_stages, ro, cs) for ro in range(1, nrow) for cs in range(ncol)]
+    row_steps = [(co.bit_length() == col_stages, co, k) for co in range(1, ncol) for k in range(pieces)]
+    order = []
+    for last in (False, True):
+        some = sorted(w for w in weights if w[0] == last)
+        order += [(last, (i + 1) / len(some), 0, (cs, ro)) for i, (_, ro, cs) in enumerate(some)]
+        some = sorted(r for r in row_steps if r[0] == last)
+        order += [(last, (i + 1) / len(some), 1, (co, k)) for i, (_, co, k) in enumerate(some)]
+    order = [entry[1:] for entry in sorted(order)]
     for _, kind, block in order:
         if kind == 0:
             weight_copy(*block).wait_recv()

time: 500 us -> 465 us (0.930)
  Pallas kernels: 401 us -> 373 us
  starting transfers between devices: 20 us -> 13.5 us
    pallas_call x1, Pallas kernels: 261 us -> 232 us  [gather(): pl.pallas_call(functools.partial(gather_kernel, split, pieces), out_shape...]
    ppermute x3, starting transfers between devices: 20 us -> 13.5 us  [swapped(): return lax.ppermute(value, 'grp', [(0, 1), (1, 0)])]
where the time goes in v4:
time: 465 us
  Pallas kernels  373 us (80%)
  matrix products  42.1 us (9%)
  local copies, waits for them, and re-layouts  29.8 us (6%)
  starting transfers between devices  13.5 us (3%)
    pallas_call x1, Pallas kernels, gather(): pl.pallas_call(functools.partial(gather_kernel, split, pieces), out_shape...  232 us
    pallas_call x1, Pallas kernels, scatter(): pl.pallas_call(functools.partial(scatter_kernel, split), out_shape=jax.Sh...  133 us
    dot_general x1, matrix products, shards(): jnp.dot(normed, w_all[:, :wide], preferred_element_type=jnp.float32)  18.2 us
    dot_general x1, matrix products, shards(): lax.dot_general(normed, chosen, (((0,), (0,)), ((), ())), preferred_eleme...  14.8 us
    ppermute x3, starting transfers between devices, swapped(): return lax.ppermute(value, 'grp', [(0, 1), (1, 0)])  13.5 us
    unnamed x23, local copies, waits for them, and re-layouts  11.4 us
  transfers between devices with their start and end apart: 3, of which 2 were waited for; matrix products, arithmetic and copies ran while one was open for 2% of the time, Pallas kernels for 0%

profile of v4, /device:TPU:0, one launch (start us, length us, event | category | flops | bytes accessed | tf_op | source)
XLA Modules:
  0.0 465.1 jit_solution(8213010326652440041)
XLA Ops:
  0.0 5.6 %fusion.20 = (bf16[1,256,1,2048]{3,2,1,0:T(2,128)(2,1)S(1)}, bf16[1,256,1,2048]{3,2,1,0:T(2,128)(2,1)S(1)}) fusion(bf16[1,256,2,2048]{3,2,1,0:T(2,128)(2,1)} %param.11), kind=kLoop, calls=%fused_computation.42 | loop fusion | bytes 4194304 | tf_op jit(solution)/shard_map/slice | solution.py:399
  5.7 0.7 slice_dynamic-update-slice_fusion.15
  6.4 1.3 copy_bitcast_fusion
  7.7 0.7 slice_dynamic-update-slice_fusion.14
  8.5 0.8 slice_dynamic-update-slice_fusion.13
  9.2 0.8 slice_dynamic-update-slice_fusion.12
  10.0 0.7 slice_dynamic-update-slice_fusion.11
  10.7 0.8 slice_dynamic-update-slice_fusion.10
  11.5 0.8 slice_dynamic-update-slice_fusion.9
  12.2 0.7 slice_dynamic-update-slice_fusion.8
  13.0 0.8 slice_dynamic-update-slice_fusion.7
  13.8 0.8 slice_dynamic-update-slice_fusion.6
  14.6 0.8 slice_dynamic-update-slice_fusion.5
  15.4 0.8 slice_dynamic-update-slice_fusion.4
  16.1 0.8 slice_dynamic-update-slice_fusion.3
  16.9 0.7 slice_dynamic-update-slice_fusion.2
  17.6 0.7 slice_dynamic-update-slice_fusion.1
  18.4 0.8 slice_dynamic-update-slice_fusion.w_ref
  19.7 2.0 fusion.6.n_ref
  21.6 232.2 %gather.1 = (bf16[4096,2048]{1,0:T(8,128)(2,1)}, bf16[1024,4096]{1,0:T(8,128)(2,1)}, bf16[1024,4096]{1,0:T(8,128)(2,1)}) custom-call(bf16[256,8192]{1,0:T(8,128)(2,1)} %slice_dynamic-update-slice_fusion.w_ref, bf16[256,4096]{1,0:T(8,128)(2,1)} %fusion.6.n_ref, bf16[256,4096]{1,0:T(8,128)(2,1)} %bitcast.20), custom_call_target="tpu_custom_call" | custom-call | tf_op jit(solution)/shard_map/gather/pallas_call | solution.py:266
  253.8 18.2 %fusion.8 = bf16[1024,1536]{1,0:T(8,128)(2,1)S(1)} fusion(bf16[1024,4096]{1,0:T(8,128)(2,1)} %get-tuple-element.10, bf16[4096,2048]{1,0:T(8,128)(2,1)} %get-tuple-element.11), kind=kOutput, calls=%fused_computation.11 | convolution fusion | flops 12886474752 | bytes 24117248 | tf_op jit(solution)/shard_map/dot_general | solution.py:407
  272.0 1.4 constant_dynamic-slice_fusion.1
  273.4 13.2 %collective-permute-start = (bf16[512,1536]{1,0:T(8,128)(2,1)}, bf16[512,1536]{1,0:T(8,128)(2,1)S(1)}, u32[]{:S(2)}, u32[]{:S(2)}) collective-permute-start(bf16[512,1536]{1,0:T(8,128)(2,1)} %get-tuple-element.15), channel_id=1, source_target_pairs={{0,16},{16,0},{1,17},{17,1},{2,18},{18,2},{3,19},{19,3},{4,20},{20... | collective-permute-start | bytes 4718600 | tf_op jit(solution)/shard_map/ppermute | solution.py:24
  286.6 9.1 %fusion.14 = bf16[1024,512]{1,0:T(8,128)(2,1)S(1)} fusion(bf16[4096,2048]{1,0:T(8,128)(2,1)} %get-tuple-element.11, bf16[1024,4096]{1,0:T(8,128)(2,1)} %get-tuple-element.10, bf16[1024,4096]{1,0:T(8,128)(2,1)} %get-tuple-element.12, pred[]{:T(512)S(6)} %eq.3), kind=kOutput, calls=%fused_computation.15 | convolution fusion | flops 4299685888 | bytes 22020096 | tf_op jit(solution)/shard_map/dot_general | solution.py:408
  295.8 1.9 collective-permute-done.1.other_last
  297.7 7.6 %attention.1 = (bf16[512,1024]{1,0:T(8,128)(2,1)S(1)}, bf16[512,1024]{1,0:T(8,128)(2,1)S(1)}) custom-call(bf16[512,1536]{1,0:T(8,128)(2,1)S(1)} %get-tuple-element.16.keep, bf16[512,512]{1,0:T(8,128)(2,1)S(1)} %get-tuple-element.22.keep_last, bf16[512,1536]{1,0:T(8,128)(2,1)S(1)} %collective-permute-done.other, ...), custom_call_target="tpu_custom_call" | custom-call | tf_op jit(solution)/shard_map/attention/pallas_call | solution.py:73
  305.6 2.5 collective-permute-done.2
  308.2 14.8 %convolution_convert_fusion.p_ref = bf16[4096,1024]{1,0:T(8,128)(2,1)} fusion(bf16[1024,4096]{1,0:T(8,128)(2,1)} %get-tuple-element.10, bf16[512,1024]{1,0:T(8,128)(2,1)S(1)} %get-tuple-element.18, bf16[512,1024]{1,0:T(8,128)(2,1)S(1)} %get-tuple-element.17), kind=kOutput, calls=%fused_computation.5 | convolution fusion | flops 8598323200 | bytes 18874368 | tf_op jit(solution)/shard_map/dot_general | solution.py:425
  323.0 132.8 %scatter.1 = bf16[4,256,1024]{2,1,0:T(8,128)(2,1)S(1)} custom-call(bf16[4096,1024]{1,0:T(8,128)(2,1)} %convolution_convert_fusion.p_ref), custom_call_target="tpu_custom_call" | custom-call | tf_op jit(solution)/shard_map/scatter/pallas_call | solution.py:368
  455.9 2.8 reshape.29
  458.6 4.3 copy.9
  462.9 2.2 reshape.30
  (15 shorter events, 1.0 us)
Async XLA Ops:
  0.0 5.7 %copy-start.1 = (bf16[1,256,2048]{2,1,0:T(8,128)(2,1)S(1)}, bf16[1,256,2048]{2,1,0:T(8,128)(2,1)}, u32[]{:S(2)}) copy-start(bf16[1,256,2048]{2,1,0:T(8,128)(2,1)} %param.9) | copy-start | bytes 3145732
  5.7 3.6 copy-start.2
  7.7 11.5 %copy-start = (bf16[1,2,128,4096]{3,2,1,0:T(8,128)(2,1)S(1)}, bf16[1,2,128,4096]{3,2,1,0:T(8,128)(2,1)}, u32[]{:S(2)}) copy-start(bf16[1,2,128,4096]{3,2,1,0:T(8,128)(2,1)} %param.6) | copy-start | bytes 6291460
  10.0 9.7 %copy-start.3 = (f32[1,4096]{1,0:T(1,128)S(1)}, f32[1,4096]{1,0:T(1,128)}, u32[]{:S(2)}) copy-start(f32[1,4096]{1,0:T(1,128)} %param.8) | copy-start | bytes 49156
  273.4 24.3 %collective-permute-start = (bf16[512,1536]{1,0:T(8,128)(2,1)}, bf16[512,1536]{1,0:T(8,128)(2,1)S(1)}, u32[]{:S(2)}, u32[]{:S(2)}) collective-permute-start(bf16[512,1536]{1,0:T(8,128)(2,1)} %get-tuple-element.15), channel_id=1, source_target_pairs={{0,16},{16,0},{1,17},{17,1},{2,18},{18,2},{3,19},{19,3},{4,20},{20... | collective-permute-start | bytes 4718600 | tf_op jit(solution)/shard_map/ppermute | solution.py:24
  295.8 2.0 collective-permute-start.1
  305.3 2.7 collective-permute-start.2

commit v5 on v4

--- a/solution.py
+++ b/solution.py
@@ -318,9 +318,11 @@
     order = list(reversed(range(ncol)))
     for ro in reversed(range(top)):
         for co in order:
-            copy = copy_of(co, top + ro)
-            copy.start()
-            copies.append(copy)
+            copies.append(copy_of(co, top + ro))
+    queue = list(copies)
+    for copy in queue[:ncol]:
+        copy.start()
+    queue = queue[ncol:]
     for stage in stages:
         bit = 1 << stage
         for ro in reversed(range(bit)):
@@ -328,6 +330,8 @@
                 copy_of(co, bit + ro).wait_recv()
                 base = slot(co, ro)
                 first = stage == stages[0]
+                if first and queue:
+                    queue.pop(0).start()
 
                 @pl.loop(0, depth // strip)
                 def _(i):

time: 465 us -> 465 us (level)
  no operation moved by 1% of the time
where the time goes in v5:
time: 465 us
  Pallas kernels  373 us (80%)
  matrix products  42.1 us (9%)
  local copies, waits for them, and re-layouts  29.8 us (6%)
  starting transfers between devices  13.5 us (3%)
    pallas_call x1, Pallas kernels, gather(): pl.pallas_call(functools.partial(gather_kernel, split, pieces), out_shape...  232 us
    pallas_call x1, Pallas kernels, scatter(): pl.pallas_call(functools.partial(scatter_kernel, split), out_shape=jax.Sh...  133 us
    dot_general x1, matrix products, shards(): jnp.dot(normed, w_all[:, :wide], preferred_element_type=jnp.float32)  18.2 us
    dot_general x1, matrix products, shards(): lax.dot_general(normed, chosen, (((0,), (0,)), ((), ())), preferred_eleme...  14.8 us
    ppermute x3, starting transfers between devices, swapped(): return lax.ppermute(value, 'grp', [(0, 1), (1, 0)])  13.5 us
    unnamed x23, local copies, waits for them, and re-layouts  11.4 us
  transfers between devices with their start and end apart: 3, of which 2 were waited for; matrix products, arithmetic and copies ran while one was open for 2% of the time, Pallas kernels for 0%

profile of v5, /device:TPU:0, one launch (start us, length us, event | category | flops | bytes accessed | tf_op | source)
XLA Modules:
  0.0 465.1 jit_solution(13928790319327627362)
XLA Ops:
  0.0 5.6 %fusion.20 = (bf16[1,256,1,2048]{3,2,1,0:T(2,128)(2,1)S(1)}, bf16[1,256,1,2048]{3,2,1,0:T(2,128)(2,1)S(1)}) fusion(bf16[1,256,2,2048]{3,2,1,0:T(2,128)(2,1)} %param.11), kind=kLoop, calls=%fused_computation.42 | loop fusion | bytes 4194304 | tf_op jit(solution)/shard_map/slice | solution.py:403
  5.7 0.7 slice_dynamic-update-slice_fusion.15
  6.4 1.3 copy_bitcast_fusion
  7.7 0.7 slice_dynamic-update-slice_fusion.14
  8.5 0.8 slice_dynamic-update-slice_fusion.13
  9.2 0.8 slice_dynamic-update-slice_fusion.12
  10.0 0.7 slice_dynamic-update-slice_fusion.11
  10.7 0.8 slice_dynamic-update-slice_fusion.10
  11.5 0.8 slice_dynamic-update-slice_fusion.9
  12.2 0.7 slice_dynamic-update-slice_fusion.8
  13.0 0.8 slice_dynamic-update-slice_fusion.7
  13.8 0.8 slice_dynamic-update-slice_fusion.6
  14.6 0.8 slice_dynamic-update-slice_fusion.5
  15.4 0.8 slice_dynamic-update-slice_fusion.4
  16.1 0.8 slice_dynamic-update-slice_fusion.3
  16.9 0.7 slice_dynamic-update-slice_fusion.2
  17.6 0.7 slice_dynamic-update-slice_fusion.1
  18.4 0.8 slice_dynamic-update-slice_fusion.w_ref
  19.7 2.0 fusion.6.n_ref
  21.6 232.2 %gather.1 = (bf16[4096,2048]{1,0:T(8,128)(2,1)}, bf16[1024,4096]{1,0:T(8,128)(2,1)}, bf16[1024,4096]{1,0:T(8,128)(2,1)}) custom-call(bf16[256,8192]{1,0:T(8,128)(2,1)} %slice_dynamic-update-slice_fusion.w_ref, bf16[256,4096]{1,0:T(8,128)(2,1)} %fusion.6.n_ref, bf16[256,4096]{1,0:T(8,128)(2,1)} %bitcast.20), custom_call_target="tpu_custom_call" | custom-call | tf_op jit(solution)/shard_map/gather/pallas_call | solution.py:266
  253.8 18.2 %fusion.8 = bf16[1024,1536]{1,0:T(8,128)(2,1)S(1)} fusion(bf16[1024,4096]{1,0:T(8,128)(2,1)} %get-tuple-element.10, bf16[4096,2048]{1,0:T(8,128)(2,1)} %get-tuple-element.11), kind=kOutput, calls=%fused_computation.11 | convolution fusion | flops 12886474752 | bytes 24117248 | tf_op jit(solution)/shard_map/dot_general | solution.py:411
  272.0 1.4 constant_dynamic-slice_fusion.1
  273.4 13.2 %collective-permute-start = (bf16[512,1536]{1,0:T(8,128)(2,1)}, bf16[512,1536]{1,0:T(8,128)(2,1)S(1)}, u32[]{:S(2)}, u32[]{:S(2)}) collective-permute-start(bf16[512,1536]{1,0:T(8,128)(2,1)} %get-tuple-element.15), channel_id=1, source_target_pairs={{0,16},{16,0},{1,17},{17,1},{2,18},{18,2},{3,19},{19,3},{4,20},{20... | collective-permute-start | bytes 4718600 | tf_op jit(solution)/shard_map/ppermute | solution.py:24
  286.6 9.1 %fusion.14 = bf16[1024,512]{1,0:T(8,128)(2,1)S(1)} fusion(bf16[4096,2048]{1,0:T(8,128)(2,1)} %get-tuple-element.11, bf16[1024,4096]{1,0:T(8,128)(2,1)} %get-tuple-element.10, bf16[1024,4096]{1,0:T(8,128)(2,1)} %get-tuple-element.12, pred[]{:T(512)S(6)} %eq.3), kind=kOutput, calls=%fused_computation.15 | convolution fusion | flops 4299685888 | bytes 22020096 | tf_op jit(solution)/shard_map/dot_general | solution.py:412
  295.8 1.9 collective-permute-done.1.other_last
  297.7 7.6 %attention.1 = (bf16[512,1024]{1,0:T(8,128)(2,1)S(1)}, bf16[512,1024]{1,0:T(8,128)(2,1)S(1)}) custom-call(bf16[512,1536]{1,0:T(8,128)(2,1)S(1)} %get-tuple-element.16.keep, bf16[512,512]{1,0:T(8,128)(2,1)S(1)} %get-tuple-element.22.keep_last, bf16[512,1536]{1,0:T(8,128)(2,1)S(1)} %collective-permute-done.other, ...), custom_call_target="tpu_custom_call" | custom-call | tf_op jit(solution)/shard_map/attention/pallas_call | solution.py:73
  305.6 2.5 collective-permute-done.2
  308.2 14.8 %convolution_convert_fusion.p_ref = bf16[4096,1024]{1,0:T(8,128)(2,1)} fusion(bf16[1024,4096]{1,0:T(8,128)(2,1)} %get-tuple-element.10, bf16[512,1024]{1,0:T(8,128)(2,1)S(1)} %get-tuple-element.18, bf16[512,1024]{1,0:T(8,128)(2,1)S(1)} %get-tuple-element.17), kind=kOutput, calls=%fused_computation.5 | convolution fusion | flops 8598323200 | bytes 18874368 | tf_op jit(solution)/shard_map/dot_general | solution.py:429
  323.0 132.8 %scatter.1 = bf16[4,256,1024]{2,1,0:T(8,128)(2,1)S(1)} custom-call(bf16[4096,1024]{1,0:T(8,128)(2,1)} %convolution_convert_fusion.p_ref), custom_call_target="tpu_custom_call" | custom-call | tf_op jit(solution)/shard_map/scatter/pallas_call | solution.py:372
  455.9 2.8 reshape.29
  458.6 4.3 copy.9
  462.9 2.2 reshape.30
  (15 shorter events, 1.0 us)
Async XLA Ops:
  0.0 5.7 %copy-start.1 = (bf16[1,256,2048]{2,1,0:T(8,128)(2,1)S(1)}, bf16[1,256,2048]{2,1,0:T(8,128)(2,1)}, u32[]{:S(2)}) copy-start(bf16[1,256,2048]{2,1,0:T(8,128)(2,1)} %param.9) | copy-start | bytes 3145732
  5.7 3.6 copy-start.2
  7.7 11.5 %copy-start = (bf16[1,2,128,4096]{3,2,1,0:T(8,128)(2,1)S(1)}, bf16[1,2,128,4096]{3,2,1,0:T(8,128)(2,1)}, u32[]{:S(2)}) copy-start(bf16[1,2,128,4096]{3,2,1,0:T(8,128)(2,1)} %param.6) | copy-start | bytes 6291460
  10.0 9.7 %copy-start.3 = (f32[1,4096]{1,0:T(1,128)S(1)}, f32[1,4096]{1,0:T(1,128)}, u32[]{:S(2)}) copy-start(f32[1,4096]{1,0:T(1,128)} %param.8) | copy-start | bytes 49156
  273.4 24.3 %collective-permute-start = (bf16[512,1536]{1,0:T(8,128)(2,1)}, bf16[512,1536]{1,0:T(8,128)(2,1)S(1)}, u32[]{:S(2)}, u32[]{:S(2)}) collective-permute-start(bf16[512,1536]{1,0:T(8,128)(2,1)} %get-tuple-element.15), channel_id=1, source_target_pairs={{0,16},{16,0},{1,17},{17,1},{2,18},{18,2},{3,19},{19,3},{4,20},{20... | collective-permute-start | bytes 4718600 | tf_op jit(solution)/shard_map/ppermute | solution.py:24
  295.8 2.0 collective-permute-start.1
  305.3 2.7 collective-permute-start.2
